TPU v7x, 32 devices: a whole 2x2x4 slice. The times are simulated.
32 devices in a mesh: dp: 8 (over z, x), ctx: 4 (over y, core).
Axes of the slice: x: 2, y: 2, z: 4, core: 2. Of those that a mesh axis runs over, the one named last changes fastest.
Arguments:
- inputs: bfloat16 [2, 8, 1024, 1024], P(None, 'dp', 'ctx'), may hold values from -6 to 6
- cotangent: bfloat16 [2, 8, 1024, 1024], P(None, 'dp', 'ctx'), may hold values from -6 to 6
- image_lengths: int32 [2, 8, 16], P(None, 'dp'), may hold values from 0 to 1024, as said below
- norm1_gain: bfloat16 [1024], replicated, may hold values from 0.25 to 1.75
- norm1_bias: bfloat16 [1024], replicated, may hold values from -1 to 1
- qkv_weight: bfloat16 [1024, 3072], replicated, may hold values from -0.1875 to 0.1875
- qv_bias: bfloat16 [2, 1024], replicated, may hold values from -1.5 to 1.5
- out_weight: bfloat16 [1024, 1024], replicated, may hold values from -0.75 to 0.75
- out_bias: bfloat16 [1024], replicated, may hold values from -1 to 1
- norm2_gain: bfloat16 [1024], replicated, may hold values from 0.25 to 1.75
- norm2_bias: bfloat16 [1024], replicated, may hold values from -1 to 1
- up_weight: bfloat16 [1024, 4096], replicated, may hold values from -0.1875 to 0.1875
- up_bias: bfloat16 [4096], replicated, may hold values from -1.5 to 1.5
- down_weight: bfloat16 [4096, 1024], replicated, may hold values from -0.09375 to 0.09375
- down_bias: bfloat16 [1024], replicated, may hold values from -1 to 1
Outputs:
- block_output: bfloat16 [2, 8, 1024, 1024], P(None, 'dp', 'ctx')
- input_grad: bfloat16 [2, 8, 1024, 1024], P(None, 'dp', 'ctx')
- grad_norm1_gain: float32 [1024], P(('dp', 'ctx'))
- grad_norm1_bias: float32 [1024], P(('dp', 'ctx'))
- grad_qkv_weight: float32 [1024, 3072], P(('dp', 'ctx'))
- grad_qv_bias: float32 [2, 1024], P(None, ('dp', 'ctx'))
- grad_out_weight: float32 [1024, 1024], P(('dp', 'ctx'))
- grad_out_bias: float32 [1024], P(('dp', 'ctx'))
- grad_norm2_gain: float32 [1024], P(('dp', 'ctx'))
- grad_norm2_bias: float32 [1024], P(('dp', 'ctx'))
- grad_up_weight: float32 [1024, 4096], P(('dp', 'ctx'))
- grad_up_bias: float32 [4096], P(('dp', 'ctx'))
- grad_down_weight: float32 [4096, 1024], P(('dp', 'ctx'))
- grad_down_bias: float32 [1024], P(('dp', 'ctx'))
Inputs may be any that keep to these rules, and one draw needn't show every extreme that they name: `image_lengths`: in each row the lengths are positive up to the row's last image and zero after it; they sum to 1024 or less, and the rest of the sequence is padding.
All inputs are finite; a program needn't handle non-finite values.
Results may differ from a plain program's by a relative error of at most 0.015.
Values may be sent and summed in bfloat16 or wider, within the bound.
No kernel may reach another device: no remote copies, remote signals or barrier semaphores. Data moves between devices by JAX's collectives and lax.ppermute only.
A program may use at most 256 MiB of HBM per device.

v0:
```python
import jax
import jax.numpy as jnp
from jax import lax
from jax.sharding import PartitionSpec as P

HEADS = 16
HEAD_DIM = 64


NEG = -1e30
EPS = 1e-06


def from_behind(value, axis, steps):
    count = lax.axis_size(axis)
    pairs = [(source, (source + steps) % count) for source in range(count)]
    return lax.ppermute(value, axis, pairs)


def norm_rows(values, gain, shift):
    centred = values - jnp.mean(values, axis=-1, keepdims=True)
    inverse = lax.rsqrt(jnp.mean(centred * centred, axis=-1, keepdims=True) + EPS)
    normal = centred * inverse
    return (normal * gain + shift, normal, inverse)


def norm_back(grad, normal, inverse, gain):
    scaled = grad * gain
    inner = (
        scaled
        - jnp.mean(scaled, axis=-1, keepdims=True)
        - normal * jnp.mean(scaled * normal, axis=-1, keepdims=True)
    )
    return (inverse * inner, jnp.sum(grad * normal, axis=0), jnp.sum(grad, axis=0))


def segments_of(lengths, positions):
    ends = jnp.cumsum(lengths, axis=-1)
    return jnp.sum((positions[None, None, :] >= ends[:, :, None]).astype(jnp.int32), axis=1)


def allowed_of(seg_rows, seg_keys, limit):
    same = seg_rows[:, None, :, None] == seg_keys[:, None, None, :]
    return same & (seg_rows[:, None, :, None] < limit)


def score_block(query, keys, allowed, scale):
    scores = jnp.einsum("bqhd,bkhd->bhqk", query, keys, preferred_element_type=jnp.float32) * scale
    return jnp.where(allowed, scores, NEG)


def add_keys(query, seg_rows, lengths, limit, scale, carry, piece):
    run_max, run_total, run_acc = carry
    keys, values = piece
    seg_keys = segments_of(lengths, jnp.arange(keys.shape[1], dtype=jnp.int32))
    allowed = allowed_of(seg_rows, seg_keys, limit)
    scores = score_block(query, keys, allowed, scale)
    new_max = jnp.maximum(run_max, jnp.max(scores, axis=-1))
    weights = jnp.where(allowed, jnp.exp(scores - new_max[..., None]), 0.0)
    run_total = jnp.sum(weights, axis=-1)
    run_acc = jnp.einsum(
        "bhqk,bkhd->bhqd", weights.astype(jnp.bfloat16), values, preferred_element_type=jnp.float32
    )
    return (new_max, run_total, run_acc)


def attend_back(query, keys, values, grad_out, row_lse, delta, allowed, scale):
    scores = score_block(query, keys, allowed, scale)
    chances = jnp.exp(jnp.where(allowed, scores - row_lse[..., None], NEG))
    d_chances = jnp.einsum("bqhd,bkhd->bhqk", grad_out, values, preferred_element_type=jnp.float32)
    d_scores = (chances * (d_chances - delta[..., None])).astype(jnp.bfloat16)
    d_query = (
        jnp.einsum("bhqk,bkhd->bqhd", d_scores, keys, preferred_element_type=jnp.float32) * scale
    )
    d_keys = (
        jnp.einsum("bhqk,bqhd->bkhd", d_scores, query, preferred_element_type=jnp.float32) * scale
    )
    d_values = jnp.einsum(
        "bhqk,bqhd->bkhd",
        chances.astype(jnp.bfloat16),
        grad_out,
        preferred_element_type=jnp.float32,
    )
    return (d_query, d_keys, d_values)


def body(
    inputs,
    cotangent,
    image_lengths,
    norm1_gain,
    norm1_bias,
    qkv_weight,
    qv_bias,
    out_weight,
    out_bias,
    norm2_gain,
    norm2_bias,
    up_weight,
    up_bias,
    down_weight,
    down_bias,
):
    micro_count, packs, seq_rows, width = inputs.shape
    limit = image_lengths.shape[-1]
    ctx_size = lax.axis_size("ctx")
    ctx_index = lax.axis_index("ctx")
    scale = HEAD_DIM ** (-0.5)
    head_shape = (packs, seq_rows, HEADS, HEAD_DIM)
    own_positions = ctx_index * seq_rows + jnp.arange(seq_rows, dtype=jnp.int32)
    weight_list = (
        norm1_gain,
        norm1_bias,
        qkv_weight,
        qv_bias,
        out_weight,
        out_bias,
        norm2_gain,
        norm2_bias,
        up_weight,
        up_bias,
        down_weight,
        down_bias,
    )
    grad_totals = [jnp.zeros(weight_arr.shape, jnp.float32) for weight_arr in weight_list]
    outputs_list = []
    input_grads = []
    for micro_index in range(micro_count):
        lengths = image_lengths[micro_index]
        seg_rows = segments_of(lengths, own_positions)
        flat_rows = inputs[micro_index].astype(jnp.float32).reshape(packs * seq_rows, width)
        normed1, normal1, inverse1 = norm_rows(flat_rows, norm1_gain, norm1_bias)
        hidden1 = normed1.astype(jnp.bfloat16)
        qkv = jnp.dot(hidden1, qkv_weight, preferred_element_type=jnp.float32)
        query4 = (qkv[:, :width] + qv_bias[0]).astype(jnp.bfloat16).reshape(head_shape)
        key4 = qkv[:, width : 2 * width].astype(jnp.bfloat16).reshape(head_shape)
        value4 = (qkv[:, 2 * width :] + qv_bias[1]).astype(jnp.bfloat16).reshape(head_shape)
        init_state = (
            jnp.full((packs, HEADS, seq_rows), NEG, jnp.float32),
            jnp.zeros((packs, HEADS, seq_rows), jnp.float32),
            jnp.zeros((packs, HEADS, seq_rows, HEAD_DIM), jnp.float32),
        )
        run_max, run_total, run_acc = add_keys(
            query4,
            seg_rows,
            lengths,
            limit,
            scale,
            init_state,
            (
                lax.all_gather(key4, "ctx", axis=1, tiled=True),
                lax.all_gather(value4, "ctx", axis=1, tiled=True),
            ),
        )
        safe_total = jnp.where(run_total > 0, run_total, 1.0)
        mixed4 = jnp.swapaxes(run_acc / safe_total[..., None], 1, 2).astype(jnp.bfloat16)
        row_lse = run_max + jnp.log(safe_total)
        attn_rows = mixed4.reshape(packs * seq_rows, width)
        middle = (
            flat_rows
            + jnp.dot(attn_rows, out_weight, preferred_element_type=jnp.float32)
            + out_bias
        )
        normed2, normal2, inverse2 = norm_rows(middle, norm2_gain, norm2_bias)
        hidden2 = normed2.astype(jnp.bfloat16)
        upper = jnp.dot(hidden2, up_weight, preferred_element_type=jnp.float32) + up_bias
        active_value, gelu_pull = jax.vjp(
            lambda upper_in: jax.nn.gelu(upper_in, approximate=False), upper
        )
        active = active_value.astype(jnp.bfloat16)
        result = (
            middle + jnp.dot(active, down_weight, preferred_element_type=jnp.float32) + down_bias
        )
        outputs_list.append(result.astype(jnp.bfloat16).reshape(packs, seq_rows, width))
        grad_rows = cotangent[micro_index].reshape(packs * seq_rows, width)
        grad_float = grad_rows.astype(jnp.float32)
        d_active = jnp.einsum(
            "rd,fd->rf", grad_rows, down_weight, preferred_element_type=jnp.float32
        )
        grad_totals[10] = grad_totals[10] + jnp.einsum(
            "rf,rd->fd", active, grad_rows, preferred_element_type=jnp.float32
        )
        grad_totals[11] = grad_totals[11] + jnp.sum(grad_float, axis=0)
        d_upper = gelu_pull(d_active)[0].astype(jnp.bfloat16)
        grad_totals[8] = grad_totals[8] + jnp.einsum(
            "rd,rf->df", hidden2, d_upper, preferred_element_type=jnp.float32
        )
        grad_totals[9] = grad_totals[9] + jnp.sum(d_upper.astype(jnp.float32), axis=0)
        d_hidden2 = jnp.einsum("rf,df->rd", d_upper, up_weight, preferred_element_type=jnp.float32)
        d_normed2, gain2_grad, bias2_grad = norm_back(d_hidden2, normal2, inverse2, norm2_gain)
        grad_totals[6] = grad_totals[6] + gain2_grad
        grad_totals[7] = grad_totals[7] + bias2_grad
        d_middle = grad_float + d_normed2
        d_branch = d_middle.astype(jnp.bfloat16)
        grad_totals[4] = grad_totals[4] + jnp.einsum(
            "rc,rd->cd", attn_rows, d_branch, preferred_element_type=jnp.float32
        )
        grad_totals[5] = grad_totals[5] + jnp.sum(d_branch.astype(jnp.float32), axis=0)
        d_mixed4 = (
            jnp.einsum("rd,cd->rc", d_branch, out_weight, preferred_element_type=jnp.float32)
            .astype(jnp.bfloat16)
            .reshape(head_shape)
        )
        delta = jnp.swapaxes(
            jnp.sum(d_mixed4.astype(jnp.float32) * mixed4.astype(jnp.float32), axis=-1), 1, 2
        )

        def cycle_turn(turn_index, carry):
            kv_stack, grad_stack, d_query = carry
            anchor = (ctx_index - turn_index) % ctx_size
            seg_keys = segments_of(
                lengths, anchor * seq_rows + jnp.arange(seq_rows, dtype=jnp.int32)
            )
            allowed = allowed_of(seg_rows, seg_keys, limit)
            part_query, part_keys, part_values = attend_back(
                query4, kv_stack[0], kv_stack[1], d_mixed4, row_lse, delta, allowed, scale
            )
            kv_stack = from_behind(kv_stack, "ctx", 1)
            grad_stack = from_behind(
                (grad_stack + jnp.stack((part_keys, part_values))).astype(jnp.bfloat16), "ctx", 1
            ).astype(jnp.float32)
            return (kv_stack, grad_stack, d_query + part_query)

        zero_rows = jnp.zeros(head_shape, jnp.float32)
        init_carry = (jnp.stack((key4, value4)), jnp.stack((zero_rows, zero_rows)), zero_rows)
        final_kv, final_grads, d_query_all = lax.fori_loop(0, ctx_size, cycle_turn, init_carry)
        d_query4 = d_query_all.astype(jnp.bfloat16)
        d_key4 = final_grads[0].astype(jnp.bfloat16)
        d_value4 = final_grads[1].astype(jnp.bfloat16)
        d_query_rows = d_query4.reshape(packs * seq_rows, width)
        d_value_rows = d_value4.reshape(packs * seq_rows, width)
        d_qkv = jnp.concatenate(
            (d_query_rows, d_key4.reshape(packs * seq_rows, width), d_value_rows), axis=-1
        )
        grad_totals[2] = grad_totals[2] + jnp.einsum(
            "rd,re->de", hidden1, d_qkv, preferred_element_type=jnp.float32
        )
        grad_totals[3] = grad_totals[3] + jnp.stack(
            (
                jnp.sum(d_query_rows.astype(jnp.float32), axis=0),
                jnp.sum(d_value_rows.astype(jnp.float32), axis=0),
            )
        )
        d_hidden1 = jnp.einsum("re,de->rd", d_qkv, qkv_weight, preferred_element_type=jnp.float32)
        d_normed1, gain1_grad, bias1_grad = norm_back(d_hidden1, normal1, inverse1, norm1_gain)
        grad_totals[0] = grad_totals[0] + gain1_grad
        grad_totals[1] = grad_totals[1] + bias1_grad
        input_grads.append(
            (d_middle + d_normed1).astype(jnp.bfloat16).reshape(packs, seq_rows, width)
        )
    summed = (
        lax.psum_scatter(grad_totals[0], ("dp", "ctx"), scatter_dimension=0, tiled=True),
        lax.psum_scatter(grad_totals[1], ("dp", "ctx"), scatter_dimension=0, tiled=True),
        lax.psum_scatter(grad_totals[2], ("dp", "ctx"), scatter_dimension=0, tiled=True),
        lax.psum_scatter(grad_totals[3], ("dp", "ctx"), scatter_dimension=1, tiled=True),
        lax.psum_scatter(grad_totals[4], ("dp", "ctx"), scatter_dimension=0, tiled=True),
        lax.psum_scatter(grad_totals[5], ("dp", "ctx"), scatter_dimension=0, tiled=True),
        lax.psum_scatter(grad_totals[6], ("dp", "ctx"), scatter_dimension=0, tiled=True),
        lax.psum_scatter(grad_totals[7], ("dp", "ctx"), scatter_dimension=0, tiled=True),
        lax.psum_scatter(grad_totals[8], ("dp", "ctx"), scatter_dimension=0, tiled=True),
        lax.psum_scatter(grad_totals[9], ("dp", "ctx"), scatter_dimension=0, tiled=True),
        lax.psum_scatter(grad_totals[10], ("dp", "ctx"), scatter_dimension=0, tiled=True),
        lax.psum_scatter(grad_totals[11], ("dp", "ctx"), scatter_dimension=0, tiled=True),
    )
    return (
        jnp.stack(outputs_list),
        jnp.stack(input_grads),
        summed[0],
        summed[1],
        summed[2],
        summed[3],
        summed[4],
        summed[5],
        summed[6],
        summed[7],
        summed[8],
        summed[9],
        summed[10],
        summed[11],
    )


def solution(mesh):
    placed = (
        P(None, "dp", "ctx", None),
        P(None, "dp", "ctx", None),
        P(None, "dp", None),
        P(),
        P(),
        P(),
        P(),
        P(),
        P(),
        P(),
        P(),
        P(),
        P(),
        P(),
        P(),
    )
    return jax.shard_map(
        body,
        mesh=mesh,
        in_specs=placed,
        out_specs=(
            P(None, "dp", "ctx", None),
            P(None, "dp", "ctx", None),
            P(("dp", "ctx")),
            P(("dp", "ctx")),
            P(("dp", "ctx"), None),
            P(None, ("dp", "ctx")),
            P(("dp", "ctx"), None),
            P(("dp", "ctx")),
            P(("dp", "ctx")),
            P(("dp", "ctx")),
            P(("dp", "ctx"), None),
            P(("dp", "ctx")),
            P(("dp", "ctx"), None),
            P(("dp", "ctx")),
        ),
        check_vma=False,
    )
```

profile of v0, /device:TPU:0, one launch (start us, length us, event | category | flops | bytes accessed | tf_op | source)
XLA Modules:
  0.0 1337.1 jit_solution(18057932973453069268)
XLA Ops:
  49.1 5.0 fusion.49
  54.2 6.1 copy-done.3
  60.3 5.1 fusion.52
  65.4 6.1 all-gather.11.cloned.1.call-done
  71.5 8.7 divide_convert_fusion
  82.4 13.6 %all-gather.5.cloned.1.call-done = bf16[1,1024,16,64]{1,3,2,0:T(8,128)(2,1)} async-done(((bf16[1,256,16,64]{1,3,2,0:T(8,128)(2,1)}), bf16[1,1024,16,64]{1,3,2,0:T(8,128)(2,1)}) %all-gather.5.cloned.1.call-update) | async-done | bytes 2097168 | tf_op jit(solution)/shard_map/all_gather | solution.py:151
  100.9 6.2 copy-done.2
  107.1 5.1 fusion.50
  112.8 7.4 all-gather.7.cloned.1.call-done
  120.3 8.7 divide_convert_fusion.1
  130.4 17.0 %multiply_convert_fusion.2 = (bf16[256,4096]{1,0:T(8,128)(2,1)}, f32[256,4096]{1,0:T(8,128)}, f32[256,4096]{1,0:T(8,128)}) fusion(f32[4096]{0:T(1024)S(1)} %convert_element_type.427, bf16[1024,4096]{1,0:T(8,128)(2,1)} %param.30, f32[256,1024]{1,0:T(8,128)S(1)} %copy-done.9, f32[256]{0:T(256)S(1)} %add_rsqrt_fusion, f32[256]{0:T(256)S(1)} %broadcast_multiply_fusion.8, ...), kind=kOutput, calls=%fused_computation.87 | convolution fusion | flops 2218000384 | bytes 19949568 | tf_op jit(solution)/shard_map/dot_general | solution.py:166
  147.4 16.2 %multiply_convert_fusion.3 = (bf16[256,4096]{1,0:T(8,128)(2,1)}, f32[256,4096]{1,0:T(8,128)S(1)}, f32[256,4096]{1,0:T(8,128)}) fusion(f32[4096]{0:T(1024)S(1)} %convert_element_type.427, bf16[1024,4096]{1,0:T(8,128)(2,1)S(1)} %bitcast.427, f32[256,1024]{1,0:T(8,128)S(1)} %get-tuple-element.839, f32[1024]{0:T(1024)S(1)} %convert_element_type.425, ...), kind=kOutput, calls=%fused_computation.100 | convolution fusion | flops 2218000384 | bytes 19949568 | tf_op jit(solution)/shard_map/dot_general | solution.py:166
  163.6 12.5 convert_reduce_fusion.2
  176.0 6.7 fusion.180
  182.8 11.6 convert_reduce_fusion.3
  194.5 8.0 multiply_reduce_fusion.1
  211.5 150.5 %while.41 = (s32[]{:T(128)}, bf16[2,1,256,16,64]{2,4,3,1,0:T(8,128)(2,1)}, f32[2,1,256,16,64]{2,4,3,1,0:T(8,128)}, f32[1,256,16,64]{1,3,2,0:T(8,128)}, s32[1,256...) while((s32[]{:T(128)}, ...), condition=%wide.region_33.34_spmd.clone, body=%wide.region_31.33_spmd.clone.sunk | while | flops 687485184 | bytes 54254544 | solution.py:226
  225.8 12.3 collective-permute-done.3
  240.9 8.4 collective-permute-done.2
  264.6 11.1 collective-permute-done.3
  278.5 8.4 collective-permute-done.2
  302.2 11.1 collective-permute-done.3
  316.1 8.4 collective-permute-done.2
  339.8 11.1 collective-permute-done.3
  353.7 8.4 collective-permute-done.2
  369.8 150.3 %while.40 = (s32[]{:T(128)}, bf16[2,1,256,16,64]{2,4,3,1,0:T(8,128)(2,1)}, f32[2,1,256,16,64]{2,4,3,1,0:T(8,128)}, f32[1,256,16,64]{1,3,2,0:T(8,128)}, s32[1,256...) while((s32[]{:T(128)}, ...), condition=%wide.region_24.25_spmd.clone, body=%wide.region_22.24_spmd.clone.sunk | while | flops 687485184 | bytes 54254544 | solution.py:226
  383.8 12.4 collective-permute-done.1
  399.0 8.4 collective-permute-done
  422.6 11.2 collective-permute-done.1
  436.6 8.4 collective-permute-done
  460.2 11.2 collective-permute-done.1
  474.1 8.4 collective-permute-done
  497.7 11.2 collective-permute-done.1
  511.7 8.4 collective-permute-done
  524.8 5.0 convolution_add_fusion.5
  535.2 6.6 convolution_add_fusion.2
  546.9 9.9 convolution_add_fusion.1
  561.3 9.9 convolution_add_fusion
  572.2 5.1 fusion.130
  577.4 6.6 fusion.116
  584.2 40.4 %all-reduce.7 = (f32[1024]{0:T(1024)S(1)}, f32[1024]{0:T(1024)S(1)}, f32[1024]{0:T(1024)S(1)}, f32[1024]{0:T(1024)S(1)}, f32[1024]{0:T(1024)S(1)}, /*index=5*/f32[4096]{0:T(1024)S(1)}, f32[1024]{0:T(1024)S(1)}) all-reduce(f32[1024]{0:T(1024)S(1)} %add.436, f32[1024]{0:T(1024)S(1)} %add.437, ...), channel_id=2, replica_groups=mesh['dp'=8,'ctx'=4] {'dp','ctx'}, use_global_device_ids=true, to_apply=%region_38.39.clone | all-reduce | flops 10240 | bytes 81920
  628.7 6.5 fusion.98
  635.3 6.0 fusion.99
  644.2 14.6 %reduce-scatter.16.cloned.1.call-done = f32[32,2]{1,0:T(8,128)} async-done(((f32[1024,2]{1,0:T(8,128)}), f32[32,2]{1,0:T(8,128)}) %reduce-scatter.16.cloned.1.call-update) | async-done | bytes 272
  660.2 138.4 %reduce-scatter.10.cloned.1.call-done = f32[32,1024]{1,0:T(8,128)} async-done(((f32[1024,1024]{1,0:T(8,128)}), f32[32,1024]{1,0:T(8,128)}) %reduce-scatter.10.cloned.1.call-update) | async-done | bytes 131088 | tf_op jit(solution)/shard_map/reduce_scatter | solution.py:256
  798.6 158.9 %reduce-scatter.8.cloned.1.call-done = f32[32,3072]{1,0:T(8,128)} async-done(((f32[1024,3072]{1,0:T(8,128)}), f32[32,3072]{1,0:T(8,128)}) %reduce-scatter.8.cloned.1.call-update) | async-done | bytes 393232 | tf_op jit(solution)/shard_map/reduce_scatter | solution.py:254
  957.5 185.0 %reduce-scatter.12.cloned.1.call-done = f32[32,4096]{1,0:T(8,128)} async-done(((f32[1024,4096]{1,0:T(8,128)}), f32[32,4096]{1,0:T(8,128)}) %reduce-scatter.12.cloned.1.call-update) | async-done | bytes 524304 | tf_op jit(solution)/shard_map/reduce_scatter | solution.py:260
  1142.5 187.5 %reduce-scatter.14.cloned.1.call-done = f32[128,1024]{1,0:T(8,128)} async-done(((f32[4096,1024]{1,0:T(8,128)}), f32[128,1024]{1,0:T(8,128)}) %reduce-scatter.14.cloned.1.call-update) | async-done | bytes 524304 | tf_op jit(solution)/shard_map/reduce_scatter | solution.py:262
  (435 shorter events, 237.4 us)
Async XLA Ops:
  7.2 73.1 %copy-start = (bf16[1024,1024]{1,0:T(8,128)(2,1)S(1)}, bf16[1024,1024]{1,0:T(8,128)(2,1)}, u32[]{:S(2)}) copy-start(bf16[1024,1024]{1,0:T(8,128)(2,1)} %param.26) | copy-start | bytes 6291460
  7.2 41.9 %all-gather.9.cloned.1.call-start = ((), (), s32[]{:S(2)}) async-start(), calls=%async_computation.7 | async-start | bytes 2621440 | tf_op jit(solution)/shard_map/all_gather | solution.py:151
  8.8 12.7 copy-start.52
  11.1 10.4 copy-start.46
  11.8 9.7 copy-start.42
  11.8 9.7 copy-start.6
  21.4 50.1 %all-gather.11.cloned.1.call-start = ((), (), s32[]{:S(2)}) async-start(), calls=%async_computation.8 | async-start | bytes 2621440 | tf_op jit(solution)/shard_map/all_gather | solution.py:152
  28.8 11.5 copy-start.77
  28.8 11.5 copy-start.83
  28.8 11.5 copy-start.84
  30.9 65.0 %all-gather.5.cloned.1.call-start = ((), (), s32[]{:S(2)}) async-start(), calls=%async_computation.5 | async-start | bytes 2621440 | tf_op jit(solution)/shard_map/all_gather | solution.py:151
  35.2 85.1 %all-gather.7.cloned.1.call-start = ((), (), s32[]{:S(2)}) async-start(), calls=%async_computation.6 | async-start | bytes 2621440 | tf_op jit(solution)/shard_map/all_gather | solution.py:152
  37.3 621.6 %reduce-scatter.16.cloned.1.call-start = ((), (), s32[]{:S(2)}) async-start(), calls=%async_computation.13 | async-start | bytes 540672
  38.2 10.9 copy-start.50
  40.3 107.0 %copy-start.48 = (f32[1024]{0:T(1024)}, f32[1024]{0:T(1024)S(1)}, u32[]{:S(2)}) copy-start(f32[1024]{0:T(1024)S(1)} %convert_element_type.425) | copy-start | bytes 12292
  40.3 162.2 %copy-start.44 = (f32[1024]{0:T(1024)}, f32[1024]{0:T(1024)S(1)}, u32[]{:S(2)}) copy-start(f32[1024]{0:T(1024)S(1)} %convert_element_type.424) | copy-start | bytes 12292
  49.1 11.2 copy-start.22
  81.1 121.4 %copy-start.58 = (f32[256]{0:T(256)}, f32[256]{0:T(256)S(1)}, u32[]{:S(2)}) copy-start(f32[256]{0:T(256)S(1)} %broadcast_multiply_fusion.8) | copy-start | bytes 3076
  82.4 120.2 %copy-start.75 = (f32[256]{0:T(256)}, f32[256]{0:T(256)S(1)}, u32[]{:S(2)}) copy-start(f32[256]{0:T(256)S(1)} %add_rsqrt_fusion) | copy-start | bytes 3076
  128.9 77.0 %copy-start.20 = (bf16[16,256,64]{1,2,0:T(8,128)(2,1)}, bf16[16,256,64]{1,2,0:T(8,128)(2,1)S(1)}, u32[]{:S(2)}) copy-start(bf16[16,256,64]{1,2,0:T(8,128)(2,1)S(1)} %divide_convert_fusion.1) | copy-start | bytes 1572868
  128.9 18.4 %slice-start = ((s8[8388608]{0:T(1024)(128)(4,1)}), s8[4194304]{0:T(1024)(128)(4,1)S(1)}, s32[]{:S(2)}) async-start(s8[8388608]{0:T(1024)(128)(4,1)} %bitcast.426), calls=%async_computation.14 | async-start | bytes 8388608
  129.8 72.8 %copy-start.11 = (f32[256,1024]{1,0:T(8,128)}, f32[256,1024]{1,0:T(8,128)S(1)}, u32[]{:S(2)}) copy-start(f32[256,1024]{1,0:T(8,128)S(1)} %get-tuple-element.839) | copy-start | bytes 3145732
  129.8 72.8 %copy-start.54 = (f32[256]{0:T(256)}, f32[256]{0:T(256)S(1)}, u32[]{:S(2)}) copy-start(f32[256]{0:T(256)S(1)} %broadcast_multiply_fusion.10) | copy-start | bytes 3076
  130.4 72.2 %copy-start.62 = (f32[256]{0:T(256)}, f32[256]{0:T(256)S(1)}, u32[]{:S(2)}) copy-start(f32[256]{0:T(256)S(1)} %add_rsqrt_fusion.2) | copy-start | bytes 3076
  130.4 17.0 %slice-start.1 = ((s8[8388608]{0:T(1024)(128)(4,1)}), s8[4194304]{0:T(1024)(128)(4,1)S(1)}, s32[]{:S(2)}) async-start(s8[8388608]{0:T(1024)(128)(4,1)} %bitcast.426), calls=%async_computation.15 | async-start | bytes 8388608
  147.3 16.2 %copy-start.21 = (bf16[2,1,256,1024]{3,2,1,0:T(8,128)(2,1)S(1)}, bf16[2,1,256,1024]{3,2,1,0:T(8,128)(2,1)}, u32[]{:S(2)}) copy-start(bf16[2,1,256,1024]{3,2,1,0:T(8,128)(2,1)} %param.20) | copy-start | bytes 3145732
  223.6 14.5 %collective-permute-start.3 = (bf16[2,1,256,16,64]{2,4,3,1,0:T(8,128)(2,1)}, bf16[2,1,256,16,64]{2,4,3,1,0:T(8,128)(2,1)}, u32[]{:S(2)}, u32[]{:S(2)}) collective-permute-start(bf16[2,1,256,16,64]{2,4,3,1,0:T(8,128)(2,1)} %fusion.273), channel_id=1, source_target_pairs={{0,1},{1,2},{2,3},{3,0},{4,5},{5,6},{6,7},{7,4},{8,9},{9,10},{10,1... | collective-permute-start | bytes 3145736 | tf_op jit(solution)/shard_map/while/body/eval_jaxpr/ppermute | solution.py:17
  223.8 25.5 %collective-permute-start.2 = (bf16[2,1,256,16,64]{2,4,3,1,0:T(8,128)(2,1)S(1)}, bf16[2,1,256,16,64]{2,4,3,1,0:T(8,128)(2,1)}, u32[]{:S(2)}, u32[]{:S(2)}) collective-permute-start(bf16[2,1,256,16,64]{2,4,3,1,0:T(8,128)(2,1)S(1)} %copy.116), channel_id=1, source_target_pairs={{0,1},{1,2},{2,3},{3,0},{4,5},{5,6},{6,7},{7,4},{8,9},{9,10},{10,1... | collective-permute-start | bytes 3145736 | tf_op jit(solution)/shard_map/while/body/eval_jaxpr/ppermute | solution.py:17
  261.1 14.5 %collective-permute-start.3 = (bf16[2,1,256,16,64]{2,4,3,1,0:T(8,128)(2,1)}, bf16[2,1,256,16,64]{2,4,3,1,0:T(8,128)(2,1)}, u32[]{:S(2)}, u32[]{:S(2)}) collective-permute-start(bf16[2,1,256,16,64]{2,4,3,1,0:T(8,128)(2,1)} %fusion.273), channel_id=1, source_target_pairs={{0,1},{1,2},{2,3},{3,0},{4,5},{5,6},{6,7},{7,4},{8,9},{9,10},{10,1... | collective-permute-start | bytes 3145736 | tf_op jit(solution)/shard_map/while/body/eval_jaxpr/ppermute | solution.py:17
  261.1 25.8 %collective-permute-start.2 = (bf16[2,1,256,16,64]{2,4,3,1,0:T(8,128)(2,1)S(1)}, bf16[2,1,256,16,64]{2,4,3,1,0:T(8,128)(2,1)}, u32[]{:S(2)}, u32[]{:S(2)}) collective-permute-start(bf16[2,1,256,16,64]{2,4,3,1,0:T(8,128)(2,1)S(1)} %copy.116), channel_id=1, source_target_pairs={{0,1},{1,2},{2,3},{3,0},{4,5},{5,6},{6,7},{7,4},{8,9},{9,10},{10,1... | collective-permute-start | bytes 3145736 | tf_op jit(solution)/shard_map/while/body/eval_jaxpr/ppermute | solution.py:17
  298.7 14.5 %collective-permute-start.3 = (bf16[2,1,256,16,64]{2,4,3,1,0:T(8,128)(2,1)}, bf16[2,1,256,16,64]{2,4,3,1,0:T(8,128)(2,1)}, u32[]{:S(2)}, u32[]{:S(2)}) collective-permute-start(bf16[2,1,256,16,64]{2,4,3,1,0:T(8,128)(2,1)} %fusion.273), channel_id=1, source_target_pairs={{0,1},{1,2},{2,3},{3,0},{4,5},{5,6},{6,7},{7,4},{8,9},{9,10},{10,1... | collective-permute-start | bytes 3145736 | tf_op jit(solution)/shard_map/while/body/eval_jaxpr/ppermute | solution.py:17
  298.7 25.8 %collective-permute-start.2 = (bf16[2,1,256,16,64]{2,4,3,1,0:T(8,128)(2,1)S(1)}, bf16[2,1,256,16,64]{2,4,3,1,0:T(8,128)(2,1)}, u32[]{:S(2)}, u32[]{:S(2)}) collective-permute-start(bf16[2,1,256,16,64]{2,4,3,1,0:T(8,128)(2,1)S(1)} %copy.116), channel_id=1, source_target_pairs={{0,1},{1,2},{2,3},{3,0},{4,5},{5,6},{6,7},{7,4},{8,9},{9,10},{10,1... | collective-permute-start | bytes 3145736 | tf_op jit(solution)/shard_map/while/body/eval_jaxpr/ppermute | solution.py:17
  336.3 14.5 %collective-permute-start.3 = (bf16[2,1,256,16,64]{2,4,3,1,0:T(8,128)(2,1)}, bf16[2,1,256,16,64]{2,4,3,1,0:T(8,128)(2,1)}, u32[]{:S(2)}, u32[]{:S(2)}) collective-permute-start(bf16[2,1,256,16,64]{2,4,3,1,0:T(8,128)(2,1)} %fusion.273), channel_id=1, source_target_pairs={{0,1},{1,2},{2,3},{3,0},{4,5},{5,6},{6,7},{7,4},{8,9},{9,10},{10,1... | collective-permute-start | bytes 3145736 | tf_op jit(solution)/shard_map/while/body/eval_jaxpr/ppermute | solution.py:17
  336.3 25.8 %collective-permute-start.2 = (bf16[2,1,256,16,64]{2,4,3,1,0:T(8,128)(2,1)S(1)}, bf16[2,1,256,16,64]{2,4,3,1,0:T(8,128)(2,1)}, u32[]{:S(2)}, u32[]{:S(2)}) collective-permute-start(bf16[2,1,256,16,64]{2,4,3,1,0:T(8,128)(2,1)S(1)} %copy.116), channel_id=1, source_target_pairs={{0,1},{1,2},{2,3},{3,0},{4,5},{5,6},{6,7},{7,4},{8,9},{9,10},{10,1... | collective-permute-start | bytes 3145736 | tf_op jit(solution)/shard_map/while/body/eval_jaxpr/ppermute | solution.py:17
  381.6 14.5 %collective-permute-start.1 = (bf16[2,1,256,16,64]{2,4,3,1,0:T(8,128)(2,1)}, bf16[2,1,256,16,64]{2,4,3,1,0:T(8,128)(2,1)}, u32[]{:S(2)}, u32[]{:S(2)}) collective-permute-start(bf16[2,1,256,16,64]{2,4,3,1,0:T(8,128)(2,1)} %fusion.258), channel_id=1, source_target_pairs={{0,1},{1,2},{2,3},{3,0},{4,5},{5,6},{6,7},{7,4},{8,9},{9,10},{10,1... | collective-permute-start | bytes 3145736 | tf_op jit(solution)/shard_map/while/body/eval_jaxpr/ppermute | solution.py:17
  381.6 25.8 %collective-permute-start = (bf16[2,1,256,16,64]{2,4,3,1,0:T(8,128)(2,1)S(1)}, bf16[2,1,256,16,64]{2,4,3,1,0:T(8,128)(2,1)}, u32[]{:S(2)}, u32[]{:S(2)}) collective-permute-start(bf16[2,1,256,16,64]{2,4,3,1,0:T(8,128)(2,1)S(1)} %copy.128), channel_id=1, source_target_pairs={{0,1},{1,2},{2,3},{3,0},{4,5},{5,6},{6,7},{7,4},{8,9},{9,10},{10,1... | collective-permute-start | bytes 3145736 | tf_op jit(solution)/shard_map/while/body/eval_jaxpr/ppermute | solution.py:17
  419.2 14.5 %collective-permute-start.1 = (bf16[2,1,256,16,64]{2,4,3,1,0:T(8,128)(2,1)}, bf16[2,1,256,16,64]{2,4,3,1,0:T(8,128)(2,1)}, u32[]{:S(2)}, u32[]{:S(2)}) collective-permute-start(bf16[2,1,256,16,64]{2,4,3,1,0:T(8,128)(2,1)} %fusion.258), channel_id=1, source_target_pairs={{0,1},{1,2},{2,3},{3,0},{4,5},{5,6},{6,7},{7,4},{8,9},{9,10},{10,1... | collective-permute-start | bytes 3145736 | tf_op jit(solution)/shard_map/while/body/eval_jaxpr/ppermute | solution.py:17
  419.2 25.8 %collective-permute-start = (bf16[2,1,256,16,64]{2,4,3,1,0:T(8,128)(2,1)S(1)}, bf16[2,1,256,16,64]{2,4,3,1,0:T(8,128)(2,1)}, u32[]{:S(2)}, u32[]{:S(2)}) collective-permute-start(bf16[2,1,256,16,64]{2,4,3,1,0:T(8,128)(2,1)S(1)} %copy.128), channel_id=1, source_target_pairs={{0,1},{1,2},{2,3},{3,0},{4,5},{5,6},{6,7},{7,4},{8,9},{9,10},{10,1... | collective-permute-start | bytes 3145736 | tf_op jit(solution)/shard_map/while/body/eval_jaxpr/ppermute | solution.py:17
  456.8 14.5 %collective-permute-start.1 = (bf16[2,1,256,16,64]{2,4,3,1,0:T(8,128)(2,1)}, bf16[2,1,256,16,64]{2,4,3,1,0:T(8,128)(2,1)}, u32[]{:S(2)}, u32[]{:S(2)}) collective-permute-start(bf16[2,1,256,16,64]{2,4,3,1,0:T(8,128)(2,1)} %fusion.258), channel_id=1, source_target_pairs={{0,1},{1,2},{2,3},{3,0},{4,5},{5,6},{6,7},{7,4},{8,9},{9,10},{10,1... | collective-permute-start | bytes 3145736 | tf_op jit(solution)/shard_map/while/body/eval_jaxpr/ppermute | solution.py:17
  456.8 25.8 %collective-permute-start = (bf16[2,1,256,16,64]{2,4,3,1,0:T(8,128)(2,1)S(1)}, bf16[2,1,256,16,64]{2,4,3,1,0:T(8,128)(2,1)}, u32[]{:S(2)}, u32[]{:S(2)}) collective-permute-start(bf16[2,1,256,16,64]{2,4,3,1,0:T(8,128)(2,1)S(1)} %copy.128), channel_id=1, source_target_pairs={{0,1},{1,2},{2,3},{3,0},{4,5},{5,6},{6,7},{7,4},{8,9},{9,10},{10,1... | collective-permute-start | bytes 3145736 | tf_op jit(solution)/shard_map/while/body/eval_jaxpr/ppermute | solution.py:17
  494.4 14.5 %collective-permute-start.1 = (bf16[2,1,256,16,64]{2,4,3,1,0:T(8,128)(2,1)}, bf16[2,1,256,16,64]{2,4,3,1,0:T(8,128)(2,1)}, u32[]{:S(2)}, u32[]{:S(2)}) collective-permute-start(bf16[2,1,256,16,64]{2,4,3,1,0:T(8,128)(2,1)} %fusion.258), channel_id=1, source_target_pairs={{0,1},{1,2},{2,3},{3,0},{4,5},{5,6},{6,7},{7,4},{8,9},{9,10},{10,1... | collective-permute-start | bytes 3145736 | tf_op jit(solution)/shard_map/while/body/eval_jaxpr/ppermute | solution.py:17
  494.4 25.8 %collective-permute-start = (bf16[2,1,256,16,64]{2,4,3,1,0:T(8,128)(2,1)S(1)}, bf16[2,1,256,16,64]{2,4,3,1,0:T(8,128)(2,1)}, u32[]{:S(2)}, u32[]{:S(2)}) collective-permute-start(bf16[2,1,256,16,64]{2,4,3,1,0:T(8,128)(2,1)S(1)} %copy.128), channel_id=1, source_target_pairs={{0,1},{1,2},{2,3},{3,0},{4,5},{5,6},{6,7},{7,4},{8,9},{9,10},{10,1... | collective-permute-start | bytes 3145736 | tf_op jit(solution)/shard_map/while/body/eval_jaxpr/ppermute | solution.py:17
  521.7 11.3 copy-start.34
  524.7 273.9 %reduce-scatter.10.cloned.1.call-start = ((), (), s32[]{:S(2)}) async-start(), calls=%async_computation.10 | async-start | bytes 4325376 | tf_op jit(solution)/shard_map/reduce_scatter | solution.py:256
  529.8 427.7 %reduce-scatter.8.cloned.1.call-start = ((), (), s32[]{:S(2)}) async-start(), calls=%async_computation.9 | async-start | bytes 12976128 | tf_op jit(solution)/shard_map/reduce_scatter | solution.py:254
  541.9 600.7 %reduce-scatter.12.cloned.1.call-start = ((), (), s32[]{:S(2)}) async-start(), calls=%async_computation.11 | async-start | bytes 17301504 | tf_op jit(solution)/shard_map/reduce_scatter | solution.py:260
  556.9 773.1 %reduce-scatter.14.cloned.1.call-start = ((), (), s32[]{:S(2)}) async-start(), calls=%async_computation.12 | async-start | bytes 17301504 | tf_op jit(solution)/shard_map/reduce_scatter | solution.py:262
  642.3 687.7 %copy-start.1 = (bf16[1024,1024]{1,0:T(8,128)(2,1)S(1)}, bf16[1024,1024]{1,0:T(8,128)(2,1)}, u32[]{:S(2)}) copy-start(bf16[1024,1024]{1,0:T(8,128)(2,1)} %param.26) | copy-start | bytes 6291460
  (72 other events, 332.5 us)
Sparse Core Ops, SparseCore 0:
  21.5 25.5 all-gather.8
  48.7 22.8 all-gather.10
  73.1 22.8 all-gather.4
  97.4 22.8 all-gather.6
  524.8 134.0 reduce-scatter.15
  661.7 136.9 reduce-scatter.9
  806.3 151.2 reduce-scatter.7
  960.4 182.0 reduce-scatter.11
  1145.4 184.5 reduce-scatter.13
where the time goes:
time: 1350 us; the launch traced here: 1340 us
  waiting for transfers between devices  870 us (64%)
  matrix products  274 us (20%)
  other arithmetic  74.9 us (6%)
  local copies, waits for them, and re-layouts  56.7 us (4%)
  blocking collectives  40.4 us (3%)
  between operations  15.8 us (1%)
    reduce_scatter x1, waiting for transfers between devices, body(): lax.psum_scatter(grad_totals[10], ('dp', 'ctx'), scatter_dimension=0, til...  187 us
    reduce_scatter x1, waiting for transfers between devices, body(): lax.psum_scatter(grad_totals[8], ('dp', 'ctx'), scatter_dimension=0, tile...  185 us
    reduce_scatter x1, waiting for transfers between devices, body(): lax.psum_scatter(grad_totals[2], ('dp', 'ctx'), scatter_dimension=0, tile...  159 us
    ppermute x16, waiting for transfers between devices, from_behind(): return lax.ppermute(value, axis, pairs)  159 us
    reduce_scatter x1, waiting for transfers between devices, body(): lax.psum_scatter(grad_totals[4], ('dp', 'ctx'), scatter_dimension=0, tile...  138 us
    unnamed x1, blocking collectives  40.4 us
    dot_general x2, matrix products, body(): jnp.dot(hidden2, up_weight, preferred_element_type=jnp.float32) + up_bias  33.2 us
  transfers between devices with their start and end apart: 25, of which 24 were waited for; matrix products, arithmetic and copies ran while one was open for 13% of the time, Pallas kernels for 0%

commit v1 on v0

v1 whole, which is shorter than its diff:
```python
import functools

import jax
import jax.numpy as jnp
from jax import lax
from jax.experimental import pallas as pl
from jax.experimental.pallas import tpu as pltpu
from jax.sharding import PartitionSpec as P

HEADS = 16
HEAD_DIM = 64
NEG = -1e30
EPS = 1e-06
LOG2E = 1.4426950408889634
BF16 = jnp.bfloat16
F32 = jnp.float32
VMEM = 56 * 1024 * 1024

NT = (((1,), (1,)), ((), ()))
NN = (((1,), (0,)), ((), ()))
TN = (((0,), (0,)), ((), ()))


def dot(left, right, dims=NN):
    return lax.dot_general(left, right, dims, preferred_element_type=F32)


def attend_kernel(limit, q_ref, k_ref, v_ref, segq_ref, segk_ref, mixed_ref, inv_ref, w_ref, vt_ref):
    block, wide = q_ref.shape
    heads = wide // HEAD_DIM

    @pl.when(pl.program_id(1) == 0)
    def _():
        values = v_ref[...]
        ones = jnp.ones(values.shape, BF16)
        vt_ref[...] = jnp.concatenate([values, ones], axis=1).T

    scaled = q_ref[...].astype(F32) * (HEAD_DIM ** (-0.5) * LOG2E)
    high = scaled.astype(BF16)
    low = (scaled - high.astype(F32)).astype(BF16)
    keys = k_ref[...]
    keys = jnp.concatenate([keys, keys], axis=1)
    lane = lax.broadcasted_iota(jnp.int32, (block, wide), 1)
    segq = segq_ref[...]
    bias = jnp.where((segk_ref[...] == segq) & (segq < limit), 0.0, NEG)
    mixed_rows = []
    inv_rows = []
    for head in range(heads):
        own = (lane >= head * HEAD_DIM) & (lane < (head + 1) * HEAD_DIM)
        zero = jnp.zeros((), BF16)
        query = jnp.concatenate([jnp.where(own, high, zero), jnp.where(own, low, zero)], axis=1)
        scores = dot(keys, query, NT) + bias
        largest = jnp.max(scores, axis=0, keepdims=True)
        weights = jnp.exp2(scores - largest).astype(BF16)
        w_ref[head] = weights
        summed = dot(vt_ref[...], weights)
        inverse = jnp.where(segq < limit, 1.0 / summed[wide : wide + 1], 0.0)
        mixed_rows.append(summed[head * HEAD_DIM : (head + 1) * HEAD_DIM] * inverse)
        inv_rows.append(jnp.broadcast_to(inverse, (HEAD_DIM, block)))
    mixed_ref[...] = jnp.concatenate(mixed_rows, axis=0).T.astype(BF16)
    inv_ref[...] = jnp.concatenate(inv_rows, axis=0).T


def attend(query, keys, values, segment, limit):
    length, width = query.shape
    heads = width // HEAD_DIM
    pair = min(2, heads)
    wide = pair * HEAD_DIM
    block = min(256, length)
    tile = pl.BlockSpec((block, wide), lambda p, j: (j, p))
    whole = pl.BlockSpec((length, wide), lambda p, j: (0, p))
    return pl.pallas_call(
        functools.partial(attend_kernel, limit),
        grid=(heads // pair, length // block),
        in_specs=[
            tile,
            whole,
            whole,
            pl.BlockSpec((1, block), lambda p, j: (0, j)),
            pl.BlockSpec((length, 1), lambda p, j: (0, 0)),
        ],
        out_specs=[tile, tile, pl.BlockSpec((pair, length, block), lambda p, j: (p, 0, j))],
        out_shape=[
            jax.ShapeDtypeStruct((length, width), BF16),
            jax.ShapeDtypeStruct((length, width), F32),
            jax.ShapeDtypeStruct((heads, length, length), BF16),
        ],
        scratch_shapes=[pltpu.VMEM((2 * wide, length), BF16)],
        compiler_params=pltpu.CompilerParams(vmem_limit_bytes=VMEM),
        name="attend",
    )(query, keys, values, segment.reshape(1, length), segment.reshape(length, 1))


def attend_back_kernel(
    q_ref, k_ref, v_ref, do_ref, mixed_ref, inv_ref, w_ref, dq_ref, dk_ref, dv_ref, kt_ref, dk_sum, dv_sum
):
    block, wide = q_ref.shape
    heads = wide // HEAD_DIM
    length = k_ref.shape[0]
    step = pl.program_id(1)

    @pl.when(step == 0)
    def _():
        kt_ref[...] = k_ref[...].T
        dk_sum[...] = jnp.zeros_like(dk_sum)
        dv_sum[...] = jnp.zeros_like(dv_sum)

    grad = do_ref[...].astype(F32)
    inverse = inv_ref[...]
    product = grad * mixed_ref[...].astype(F32)
    grad = (grad * inverse).astype(BF16)
    query = q_ref[...]
    lane = lax.broadcasted_iota(jnp.int32, (block, wide), 1)
    key_lane = lax.broadcasted_iota(jnp.int32, (length, wide), 1)
    zero = jnp.zeros((), BF16)
    minus = jnp.where(key_lane < 2, -jnp.ones((), BF16), zero)
    values = jnp.concatenate([v_ref[...], minus], axis=1)
    dq_rows = []
    for head in range(heads):
        own = (lane >= head * HEAD_DIM) & (lane < (head + 1) * HEAD_DIM)
        delta = jnp.sum(jnp.where(own, product * inverse, 0.0), axis=1, keepdims=True)
        high = delta.astype(BF16)
        low = (delta - high.astype(F32)).astype(BF16)
        extra = jnp.where(lane == 0, high, jnp.where(lane == 1, low, zero))
        own_grad = jnp.where(own, grad, zero)
        weights = w_ref[head]
        d_probs = dot(values, jnp.concatenate([own_grad, extra], axis=1), NT)
        d_scores = weights * d_probs.astype(BF16)
        dv_sum[...] += dot(weights, own_grad)
        dk_sum[...] += dot(d_scores, jnp.where(own, query, zero))
        dq_rows.append(dot(kt_ref[head * HEAD_DIM : (head + 1) * HEAD_DIM], d_scores))
    scale = HEAD_DIM ** (-0.5)
    dq_ref[...] = (jnp.concatenate(dq_rows, axis=0).T * scale).astype(BF16)

    @pl.when(step == pl.num_programs(1) - 1)
    def _():
        dk_ref[...] = (dk_sum[...] * scale).astype(BF16)
        dv_ref[...] = dv_sum[...].astype(BF16)


def attend_back(query, keys, values, d_mixed, mixed, inverse, weights):
    length, width = query.shape
    heads = width // HEAD_DIM
    pair = min(2, heads)
    wide = pair * HEAD_DIM
    block = min(256, length)
    tile = pl.BlockSpec((block, wide), lambda p, j: (j, p))
    whole = pl.BlockSpec((length, wide), lambda p, j: (0, p))
    shape = jax.ShapeDtypeStruct((length, width), BF16)
    return pl.pallas_call(
        attend_back_kernel,
        grid=(heads // pair, length // block),
        in_specs=[
            tile,
            whole,
            whole,
            tile,
            tile,
            tile,
            pl.BlockSpec((pair, length, block), lambda p, j: (p, 0, j)),
        ],
        out_specs=[tile, whole, whole],
        out_shape=[shape, shape, shape],
        scratch_shapes=[
            pltpu.VMEM((wide, length), BF16),
            pltpu.VMEM((length, wide), F32),
            pltpu.VMEM((length, wide), F32),
        ],
        compiler_params=pltpu.CompilerParams(vmem_limit_bytes=VMEM),
        name="attend_back",
    )(query, keys, values, d_mixed, mixed, inverse, weights)


def feed_kernel(
    h_ref, cot_ref, up_ref, upb_ref, down_ref, active_ref, dup_ref, dub_ref, out_ref, dh_ref, out_sum, dh_sum
):
    step = pl.program_id(1)

    @pl.when(step == 0)
    def _():
        out_sum[...] = jnp.zeros_like(out_sum)
        dh_sum[...] = jnp.zeros_like(dh_sum)

    up = up_ref[...]
    down = down_ref[...]
    upper = dot(h_ref[...], up) + upb_ref[...].astype(F32)
    d_active = dot(cot_ref[...], down, NT)
    half = 0.5 + 0.5 * lax.erf(upper * 0.7071067811865476)
    bell = jnp.exp2(upper * upper * (-0.5 * LOG2E)) * 0.3989422804014327
    active = (upper * half).astype(BF16)
    d_upper = d_active * (half + upper * bell)
    d_low = d_upper.astype(BF16)
    active_ref[...] = active
    dup_ref[...] = d_low
    dub_ref[...] = jnp.sum(d_low.astype(F32), axis=0, keepdims=True)[None]
    out_sum[...] += dot(active, down)
    dh_sum[...] += dot(d_low, up, NT)

    @pl.when(step == pl.num_programs(1) - 1)
    def _():
        out_ref[...] = out_sum[...].astype(out_ref.dtype)
        dh_ref[...] = dh_sum[...].astype(dh_ref.dtype)


def feed(hidden, cotangent, up, up_bias, down):
    length, width = hidden.shape
    ff = up.shape[1]
    rows = min(length, 1024)
    tile = min(256, ff)
    row_spec = pl.BlockSpec((rows, width), lambda i, t: (i, 0))
    ff_spec = pl.BlockSpec((rows, tile), lambda i, t: (i, t))
    return pl.pallas_call(
        feed_kernel,
        grid=(length // rows, ff // tile),
        in_specs=[
            row_spec,
            row_spec,
            pl.BlockSpec((width, tile), lambda i, t: (0, t)),
            pl.BlockSpec((1, tile), lambda i, t: (0, t)),
            pl.BlockSpec((tile, width), lambda i, t: (t, 0)),
        ],
        out_specs=[
            ff_spec,
            ff_spec,
            pl.BlockSpec((1, 1, tile), lambda i, t: (i, 0, t)),
            row_spec,
            row_spec,
        ],
        out_shape=[
            jax.ShapeDtypeStruct((length, ff), BF16),
            jax.ShapeDtypeStruct((length, ff), BF16),
            jax.ShapeDtypeStruct((length // rows, 1, ff), F32),
            jax.ShapeDtypeStruct((length, width), BF16),
            jax.ShapeDtypeStruct((length, width), BF16),
        ],
        scratch_shapes=[pltpu.VMEM((rows, width), F32), pltpu.VMEM((rows, width), F32)],
        compiler_params=pltpu.CompilerParams(vmem_limit_bytes=VMEM),
        name="feed",
    )(hidden, cotangent, up, up_bias, down)


def norm_parts(values):
    centred = values - jnp.mean(values, axis=-1, keepdims=True)
    inverse = lax.rsqrt(jnp.mean(centred * centred, axis=-1, keepdims=True) + EPS)
    return centred * inverse, inverse


def norm_back(grad, normal, inverse, gain):
    scaled = grad * gain
    inner = (
        scaled
        - jnp.mean(scaled, axis=-1, keepdims=True)
        - normal * jnp.mean(scaled * normal, axis=-1, keepdims=True)
    )
    return inverse * inner


def body(
    inputs,
    cotangent,
    image_lengths,
    norm1_gain,
    norm1_bias,
    qkv_weight,
    qv_bias,
    out_weight,
    out_bias,
    norm2_gain,
    norm2_bias,
    up_weight,
    up_bias,
    down_weight,
    down_bias,
):
    rows, width = inputs.shape[2:]
    limit = image_lengths.shape[-1]
    ff = up_weight.shape[1]
    dp_size = lax.axis_size("dp")
    ctx_size = lax.axis_size("ctx")
    group = ctx_size // 2
    dp_index = lax.axis_index("dp")
    ctx_index = lax.axis_index("ctx")
    half = ctx_index // group
    member = ctx_index % group
    length = rows * ctx_size
    chips = dp_size * 2
    dp_bits = dp_size.bit_length() - 1
    own_heads = HEADS // group
    own_width = own_heads * HEAD_DIM
    block_rows = ff // (chips * group)

    def across(value):
        pairs = [(i, (i + group) % ctx_size) for i in range(ctx_size)]
        return lax.ppermute(value, "ctx", pairs)

    def around(value, steps):
        pairs = [
            (h * group + g, h * group + (g + steps) % group) for h in range(2) for g in range(group)
        ]
        return lax.ppermute(value, "ctx", pairs)

    def gather(value):
        parts = [value] + [around(value, steps) for steps in range(1, group)]
        if group == 2:
            first = member == 0
            return jnp.stack(
                [jnp.where(first, parts[0], parts[1]), jnp.where(first, parts[1], parts[0])]
            )
        stacked = jnp.stack(parts[::-1])
        return jnp.roll(stacked, member + 1, axis=0)

    def pick(value, index, axis):
        return lax.dynamic_index_in_dim(value, index, axis, keepdims=False)

    def group_sum_scatter(value, axis):
        total = pick(value, member, axis).astype(F32)
        for steps in range(1, group):
            total = total + around(pick(value, (member + steps) % group, axis), steps).astype(F32)
        return total

    def group_sum(value):
        total = value.astype(F32)
        for steps in range(1, group):
            total = total + around(value, steps).astype(F32)
        return total

    def swap_bit(value, bit):
        if bit < 0:
            return across(value)
        return lax.ppermute(value, "dp", [(i, i ^ (1 << bit)) for i in range(dp_size)])

    def bit_of(bit):
        return half if bit < 0 else (dp_index >> bit) & 1

    def chip_scatter(value, order, dtype=BF16):
        rest = value.shape[1:]
        value = value.reshape((2,) * (dp_bits + 1) + rest)
        left = list(range(dp_bits - 1, -1, -1)) + [-1]
        keep = send = None
        for number, bit in enumerate(order):
            axis = left.index(bit)
            mine = bit_of(bit)
            if number == 0:
                keep = pick(value, mine, axis)
                send = pick(value, 1 - mine, axis)
            else:
                keep, send = (
                    pick(keep, mine, axis).astype(F32) + pick(came, mine, axis).astype(F32),
                    pick(keep, 1 - mine, axis).astype(F32) + pick(came, 1 - mine, axis).astype(F32),
                )
                keep = keep.astype(dtype)
                send = send.astype(dtype)
            left.pop(axis)
            came = swap_bit(send, bit)
        return keep.astype(F32) + came.astype(F32)

    own_inputs = pick(inputs, half, 0)[0]
    other_inputs = across(pick(inputs, 1 - half, 0)[0])
    own_cot = pick(cotangent, half, 0)[0]
    other_cot = across(pick(cotangent, 1 - half, 0)[0])
    x_rows = jnp.concatenate([gather(own_inputs), gather(other_inputs)]).reshape(length, width)
    cot_rows = jnp.concatenate([gather(own_cot), gather(other_cot)]).reshape(length, width)

    place = jnp.arange(length, dtype=jnp.int32).reshape(2, length // 2)
    positions = jnp.where(half == 0, place, place[::-1]).reshape(length)
    ends = jnp.cumsum(pick(image_lengths, half, 0)[0])
    segment = jnp.sum((positions[:, None] >= ends[None, :]).astype(jnp.int32), axis=1)

    qkv_own = pick(qkv_weight.reshape(width, 3, group, own_width), member, 2).reshape(width, 3 * own_width)
    up_own = pick(up_weight.reshape(width, chips, group, block_rows), member, 2).reshape(width, ff // group)
    upb_own = pick(up_bias.reshape(chips, group, block_rows), member, 1).reshape(1, ff // group)
    down_own = pick(down_weight.reshape(chips, group, block_rows, width), member, 1).reshape(ff // group, width)
    bias_own = pick(qv_bias.reshape(2, group, own_width), member, 1)

    normal1, _ = norm_parts(x_rows.astype(F32))
    hidden1 = (normal1 * norm1_gain + norm1_bias).astype(BF16)
    qkv = dot(hidden1, qkv_own)
    query = (qkv[:, :own_width] + bias_own[0]).astype(BF16)
    keys = qkv[:, own_width : 2 * own_width].astype(BF16)
    values = (qkv[:, 2 * own_width :] + bias_own[1]).astype(BF16)
    mixed, inverse, weights = attend(query, keys, values, segment, limit)
    mixed_all = jnp.swapaxes(gather(mixed), 0, 1).reshape(length, width)
    middle = x_rows.astype(F32) + dot(mixed_all, out_weight) + out_bias
    normal2, inverse2 = norm_parts(middle)
    hidden2 = (normal2 * norm2_gain + norm2_bias).astype(BF16)
    active, d_upper, upb_grad, out_part, dh_part = feed(hidden2, cot_rows, up_own, upb_own, down_own)

    d_hidden2 = group_sum(dh_part)
    down_grad = dot(active, cot_rows, TN).astype(BF16).reshape(chips, block_rows, width)
    up_grad = dot(hidden2, d_upper, TN).astype(BF16).reshape(chips, width // chips, ff // group)

    order_a = [0] + list(range(1, dp_bits)) + [-1]
    order_b = [-1, 0] + list(range(1, dp_bits))
    order_c = list(range(1, dp_bits)) + [0, -1]

    def spread(value, cuts, orders):
        parts = []
        start = 0
        for cut, order in zip(cuts, orders):
            parts.append(chip_scatter(value[:, :, start : start + cut], order))
            start += cut
        return jnp.concatenate(parts, axis=-1) if len(parts) > 1 else parts[0]

    def thirds(columns):
        first = columns * 3 // 8 // 128 * 128
        if first == 0:
            return [columns], [order_a]
        return [first, first, columns - 2 * first], [order_a, order_b, order_c]

    down_total = spread(down_grad, *thirds(width))
    up_total = spread(up_grad, *thirds(ff // group))

    own_rows = (2, group, rows, width)
    out_sum = group_sum_scatter(out_part.reshape(own_rows), 1)
    middle_own = pick(middle.reshape(own_rows), member, 1)
    result = (out_sum + middle_own + down_bias).astype(BF16)

    def hand_back(value):
        came = across(value[1])
        first = half == 0
        return jnp.stack(
            [jnp.where(first, value[0], came), jnp.where(first, came, value[0])]
        )[:, None]

    block_output = hand_back(result)

    d_middle = cot_rows.astype(F32) + norm_back(d_hidden2, normal2, inverse2, norm2_gain)
    d_branch = d_middle.astype(BF16)
    wo_own = pick(out_weight.reshape(group, own_width, width), member, 0)
    d_mixed = dot(d_branch, wo_own, NT).astype(BF16)
    d_branch_own = pick(d_branch.reshape(length, group, width // group), member, 1)
    out_grad = dot(mixed_all, d_branch_own, TN).astype(BF16).reshape(chips, width // chips, width // group)
    out_total = spread(out_grad, [width // group], [order_c])
    d_query, d_keys, d_values = attend_back(query, keys, values, d_mixed, mixed, inverse, weights)
    d_qkv = jnp.concatenate([d_query, d_keys, d_values], axis=1)
    qkv_grad = dot(hidden1, d_qkv, TN).astype(BF16).reshape(chips, width // chips, 3 * own_width)
    qkv_total = spread(qkv_grad, *thirds(3 * own_width))
    dh1_part = dot(d_qkv, qkv_own, NT).astype(BF16)
    d_hidden1 = group_sum_scatter(dh1_part.reshape(own_rows), 1)
    x_own = pick(x_rows.reshape(own_rows), member, 1).astype(F32)
    n1_own, i1_own = norm_parts(x_own)
    d_middle_own = pick(d_middle.reshape(own_rows), member, 1)
    input_grad = hand_back((d_middle_own + norm_back(d_hidden1, n1_own, i1_own, norm1_gain)).astype(BF16))

    both = 1.0 / group
    member_is = (jnp.arange(group, dtype=jnp.int32) == member).astype(F32)

    def at_member(vector):
        return (member_is[:, None] * vector[None, :]).reshape(-1)

    upb_sum = jnp.sum(upb_grad, axis=(0, 1)).reshape(chips, 1, block_rows)
    upb_full = (member_is[None, :, None] * upb_sum).reshape(chips, group, block_rows)
    vectors = [
        jnp.sum(d_hidden1 * n1_own, axis=(0, 1)),
        jnp.sum(d_hidden1, axis=(0, 1)),
        at_member(jnp.sum(d_query.astype(F32), axis=0)),
        at_member(jnp.sum(d_values.astype(F32), axis=0)),
        jnp.sum(d_branch.astype(F32), axis=0) * both,
        jnp.sum(d_hidden2 * normal2, axis=0) * both,
        jnp.sum(d_hidden2, axis=0) * both,
        jnp.sum(cotangent[:, 0].astype(F32), axis=(0, 1)),
    ]
    small = jnp.stack(vectors).reshape(len(vectors), chips, group, width // (chips * group))
    small = jnp.transpose(small, (1, 2, 0, 3)).reshape(chips, group, -1)
    small = jnp.concatenate([small, upb_full], axis=-1)
    small = chip_scatter(small, order_a, F32)
    small = group_sum_scatter(small, 0)
    own_cols = width // (chips * group)
    small_rows = small[: len(vectors) * own_cols].reshape(len(vectors), own_cols)
    upb_out = small[len(vectors) * own_cols :]

    def exchange(value):
        own = value.shape[0] // group
        value = value.reshape(group, own, value.shape[1])
        parts = [pick(value, member, 0)] + [
            around(pick(value, (member + steps) % group, 0).astype(BF16), steps).astype(F32)
            for steps in range(1, group)
        ]
        if group == 2:
            first = member == 0
            return jnp.stack(
                [jnp.where(first, parts[0], parts[1]), jnp.where(first, parts[1], parts[0])], axis=1
            )
        return jnp.swapaxes(jnp.roll(jnp.stack(parts[::-1]), member + 1, axis=0), 0, 1)

    own = width // (chips * group)
    up_out = exchange(up_total).reshape(own, group, chips, block_rows)
    up_out = jnp.swapaxes(up_out, 1, 2).reshape(own, ff)
    qkv_out = exchange(qkv_total).reshape(own, group, 3, own_width)
    qkv_out = jnp.swapaxes(qkv_out, 1, 2).reshape(own, 3 * width)
    out_out = exchange(out_total).reshape(own, width)
    return (
        block_output,
        input_grad,
        small_rows[0],
        small_rows[1],
        qkv_out,
        small_rows[2:4],
        out_out,
        small_rows[4],
        small_rows[5],
        small_rows[6],
        up_out,
        upb_out,
        down_total,
        small_rows[7],
    )


def solution(mesh):
    split = P(None, "dp", "ctx", None)
    both = ("dp", "ctx")
    return jax.shard_map(
        body,
        mesh=mesh,
        in_specs=(split, split, P(None, "dp", None)) + (P(),) * 12,
        out_specs=(
            split,
            split,
            P(both),
            P(both),
            P(both, None),
            P(None, both),
            P(both, None),
            P(both),
            P(both),
            P(both),
            P(both, None),
            P(both),
            P(both, None),
            P(both),
        ),
        check_vma=False,
    )
```

time: 1350 us -> 466 us (0.35)
  waiting for transfers between devices: 870 us -> 110 us
  matrix products: 274 us -> 34.7 us
  Pallas kernels: 0 us -> 88.4 us
  local copies, waits for them, and re-layouts: 56.7 us -> 113 us
  starting transfers between devices: 4.27 us -> 58.9 us
  blocking collectives: 40.4 us -> 0 us
  other arithmetic: 74.9 us -> 54 us
  between operations: 15.8 us -> 2.25 us
    reduce_scatter x4 -> x0, waiting for transfers between devices: 670 us -> none  [the longest x1 187 us: body(): lax.psum_scatter(grad_totals[10], ('dp', 'ctx'), scatter_dimension=0, til...]
    dot_general x68 -> x8, matrix products: 274 us -> 34.7 us  [dot(): return lax.dot_general(left, right, dims, preferred_element_type=F32)]
    pallas_call x0 -> x3, Pallas kernels: none -> 88.4 us  [the longest x1 34.2 us: attend(): pl.pallas_call(functools.partial(attend_kernel, limit), grid=(heads // pa...]
    ppermute x16 -> x60, starting transfers between devices: 3.44 us -> 58.9 us  [the longest x33 39.6 us: swap_bit(): lax.ppermute(value, 'dp', [(i, i ^ 1 << bit) for i in range(dp_size)])]
    ppermute x16 -> x60, waiting for transfers between devices: 159 us -> 110 us  [the longest x33 94.6 us: swap_bit(): lax.ppermute(value, 'dp', [(i, i ^ 1 << bit) for i in range(dp_size)])]
    unnamed x1 -> x0, blocking collectives: 40.4 us -> none
    dynamic_slice x0 -> x5, local copies, waits for them, and re-layouts: none -> 39.2 us  [pick(): return lax.dynamic_index_in_dim(value, index, axis, keepdims=False)]
    all_gather x4 -> x0, waiting for transfers between devices: 27.2 us -> none  [the longest x2 13.6 us: body(): lax.all_gather(key4, 'ctx', axis=1, tiled=True)]
  transfers between devices with their start and end apart: 25 -> 60, of which waited for: 24 -> 24; matrix products, arithmetic and copies ran while one was open for 13% -> 30% of each run, Pallas kernels for 0% -> 7%
where the time goes in v1:
time: 466 us; the launch traced here: 461 us
  local copies, waits for them, and re-layouts  113 us (24%)
  waiting for transfers between devices  110 us (24%)
  Pallas kernels  88.4 us (19%)
  starting transfers between devices  58.9 us (13%)
  other arithmetic  54 us (12%)
  matrix products  34.7 us (7%)
    ppermute x33, waiting for transfers between devices, swap_bit(): lax.ppermute(value, 'dp', [(i, i ^ 1 << bit) for i in range(dp_size)])  94.6 us
    ppermute x33, starting transfers between devices, swap_bit(): lax.ppermute(value, 'dp', [(i, i ^ 1 << bit) for i in range(dp_size)])  39.6 us
    dynamic_slice x5, local copies, waits for them, and re-layouts, pick(): return lax.dynamic_index_in_dim(value, index, axis, keepdims=False)  39.2 us
    dot_general x8, matrix products, dot(): return lax.dot_general(left, right, dims, preferred_element_type=F32)  34.7 us
    pallas_call x1, Pallas kernels, attend(): pl.pallas_call(functools.partial(attend_kernel, limit), grid=(heads // pa...  34.2 us
    pallas_call x1, Pallas kernels, feed(): pl.pallas_call(feed_kernel, grid=(length // rows, ff // tile), in_specs=[...  28 us
    pallas_call x1, Pallas kernels, attend_back(): pl.pallas_call(attend_back_kernel, grid=(heads // pair, length // block),...  26.1 us
    unnamed x98, local copies, waits for them, and re-layouts  22.9 us
  transfers between devices with their start and end apart: 60, of which 24 were waited for; matrix products, arithmetic and copies ran while one was open for 30% of the time, Pallas kernels for 7%

profile of v1, /device:TPU:0, one launch (start us, length us, event | category | flops | bytes accessed | tf_op | source)
XLA Modules:
  0.0 460.6 jit_solution(12503582777061645636)
XLA Ops:
  0.7 2.4 dynamic-slice_bitcast_fusion.9
  3.6 2.5 collective-permute-start.1
  7.6 8.7 %copy.101 = bf16[1024,3072]{0,1:T(8,128)(2,1)} copy(bf16[1024,3072]{1,0:T(8,128)(2,1)} %param.20) | data formatting | bytes 12582912 | tf_op args[5]
  16.7 14.3 %reshape.922 = bf16[1024,16,2,128]{3,2,1,0:T(2,128)(2,1)} reshape(bf16[1024,4096]{1,0:T(8,128)(2,1)} %param.26) | data formatting | bytes 16777216 | tf_op jit(solution)/shard_map/reshape | solution.py:370
  31.0 28.4 %dynamic-slice_reduce_fusion = bf16[1024,16,128]{2,1,0:T(8,128)(2,1)} fusion(bf16[1024,16,2,128]{3,2,1,0:T(2,128)(2,1)} %reshape.922, s32[]{:T(128)S(6)} %select_n.407), kind=kLoop, calls=%fused_computation | loop fusion | bytes 8388612 | tf_op jit(solution)/shard_map/jit(dynamic_index_in_dim)/dynamic_slice | solution.py:313
  59.3 4.8 %constant_dynamic-slice_fusion.23 = bf16[16,1,128,1024]{3,2,1,0:T(8,128)(2,1)} fusion(bf16[16,2,128,1024]{3,2,1,0:T(8,128)(2,1)} %bitcast.616, s32[]{:T(128)S(6)} %select_n.407), kind=kLoop, calls=%fused_computation.293 | loop fusion | bytes 8388612 | tf_op jit(solution)/shard_map/jit(dynamic_index_in_dim)/dynamic_slice | solution.py:313
  64.3 3.9 constant_dynamic-slice_fusion.27
  69.3 6.3 %copy.158 = bf16[128,8,16,128]{3,1,2,0:T(8,128)(2,1)} copy(bf16[128,8,16,128]{3,2,1,0:T(8,128)(2,1)} %bitcast.583) | data formatting | bytes 8388608
  84.3 3.4 fusion.143
  90.8 34.2 %attend.1 = (bf16[1024,512]{1,0:T(8,128)(2,1)}, f32[1024,512]{1,0:T(8,128)}, bf16[8,1024,1024]{2,1,0:T(8,128)(2,1)}) custom-call(bf16[1024,512]{1,0:T(8,128)(2,1)} %get-tuple-element.94.q_ref, bf16[1024,512]{1,0:T(8,128)(2,1)} %slice.172.k_ref, bf16[1024,512]{1,0:T(8,128)(2,1)} %get-tuple-element.93.v_ref, s32[1,1024]{1,0:T(1,128)} %bitcast.636, ...), custom_call_target="tpu_custom_call" | custom-call | tf_op jit(solution)/shard_map/attend/pallas_call | solution.py:72
  133.2 4.0 copy.104
  137.1 4.9 %fusion.142 = (f32[1024]{0:T(1024)S(1)}, f32[1024,1024]{1,0:T(8,128)S(1)}) fusion(f32[1024]{0:T(1024)S(1)} %convert_element_type.1180, bf16[1024,1024]{0,1:T(8,128)(2,1)} %bitcast.617, bf16[1024,1024]{1,0:T(8,128)(2,1)S(1)} %copy-done, bf16[4,256,1024]{2,1,0:T(8,128)(2,1)} %copy-done.3), kind=kOutput, calls=%fused_computation.351 | convolution fusion | flops 2151676928 | bytes 10493952 | tf_op jit(solution)/shard_map/dot_general | solution.py:25
  144.7 28.0 %feed.1 = (bf16[1024,2048]{1,0:T(8,128)(2,1)}, bf16[1024,2048]{1,0:T(8,128)(2,1)}, f32[1,1,2048]{2,1,0:T(1,128)}, bf16[1024,1024]{1,0:T(8,128)(2,1)}, bf16[1024,1024]{1,0:T(8,128)(2,1)}) custom-call(bf16[1024,1024]{1,0:T(8,128)(2,1)} %add_convert_fusion.h_ref, bf16[1024,1024]{1,0:T(8,128)(2,1)} %bitcast.581, bf16[1024,2048]{1,0:T(8,128)(2,1)} %bitcast.585, ...), custom_call_target="tpu_custom_call" | custom-call | tf_op jit(solution)/shard_map/feed/pallas_call | solution.py:212
  172.8 7.4 %convolution_convert_fusion.1 = bf16[2048,1024]{1,0:T(8,128)(2,1)S(1)} fusion(bf16[1024,2048]{1,0:T(8,128)(2,1)} %get-tuple-element.35, bf16[1024,1024]{1,0:T(8,128)(2,1)} %bitcast.582), kind=kOutput, calls=%fused_computation.26 | convolution fusion | flops 4297064448 | bytes 10485760 | tf_op jit(solution)/shard_map/dot_general | solution.py:25
  183.2 5.1 %convolution_convert_fusion.2 = bf16[1024,2048]{1,0:T(8,128)(2,1)S(1)} fusion(bf16[1024,1024]{1,0:T(8,128)(2,1)S(1)} %copy-done.6, bf16[1024,2048]{1,0:T(8,128)(2,1)S(1)} %copy-done.43), kind=kOutput, calls=%fused_computation.27 | convolution fusion | flops 4297064448 | bytes 10485760 | tf_op jit(solution)/shard_map/dot_general | solution.py:25
  195.7 11.9 %collective-permute-done.56 = bf16[2,2,2,128,256]{4,3,2,1,0:T(8,128)(2,1)S(1)} collective-permute-done((bf16[2,2,2,128,256]{4,3,2,1,0:T(8,128)(2,1)S(1)}, bf16[2,2,2,128,256]{4,3,2,1,0:T(8,128)(2,1)S(1)}, u32[]{:S(2)}, u32[]{:S(2)}) %collective-permute-start.56) | collective-permute-done | bytes 524320 | tf_op jit(solution)/shard_map/ppermute | solution.py:330
  208.3 9.1 %collective-permute-done.43 = bf16[2,2,2,64,512]{4,3,2,1,0:T(8,128)(2,1)S(1)} collective-permute-done((bf16[2,2,2,64,512]{4,3,2,1,0:T(8,128)(2,1)S(1)}, bf16[2,2,2,64,512]{4,3,2,1,0:T(8,128)(2,1)S(1)}, u32[]{:S(2)}, u32[]{:S(2)}) %collective-permute-start.43) | collective-permute-done | bytes 524320 | tf_op jit(solution)/shard_map/ppermute | solution.py:330
  217.3 2.6 collective-permute-start.57
  220.2 10.5 %collective-permute-done.57 = bf16[2,2,128,256]{3,2,1,0:T(8,128)(2,1)S(1)} collective-permute-done((bf16[2,2,128,256]{3,2,1,0:T(8,128)(2,1)S(1)}, bf16[2,2,128,256]{3,2,1,0:T(8,128)(2,1)S(1)}, u32[]{:S(2)}, u32[]{:S(2)}) %collective-permute-start.57) | collective-permute-done | bytes 262176 | tf_op jit(solution)/shard_map/ppermute | solution.py:330
  231.8 14.2 %collective-permute-done.44 = bf16[2,2,64,512]{3,2,1,0:T(8,128)(2,1)S(1)} collective-permute-done((bf16[2,2,64,512]{3,2,1,0:T(8,128)(2,1)S(1)}, bf16[2,2,64,512]{3,2,1,0:T(8,128)(2,1)S(1)}, u32[]{:S(2)}, u32[]{:S(2)}) %collective-permute-start.44) | collective-permute-done | bytes 262176 | tf_op jit(solution)/shard_map/ppermute | solution.py:330
  248.7 3.9 collective-permute-done.58
  255.9 4.4 collective-permute-done.59
  260.9 3.7 collective-permute-done.46
  268.5 10.3 %collective-permute-done.36 = bf16[2,2,64,768]{3,2,1,0:T(8,128)(2,1)S(1)} collective-permute-done((bf16[2,2,64,768]{3,2,1,0:T(8,128)(2,1)S(1)}, bf16[2,2,64,768]{3,2,1,0:T(8,128)(2,1)S(1)}, u32[]{:S(2)}, u32[]{:S(2)}) %collective-permute-start.36) | collective-permute-done | bytes 393248 | tf_op jit(solution)/shard_map/ppermute | solution.py:330
  278.9 2.8 collective-permute-start.37
  282.9 3.0 collective-permute-done.54
  285.9 2.4 collective-permute-start.51
  288.4 2.5 collective-permute-done.37
  293.2 2.6 collective-permute-done.38
  295.8 2.9 collective-permute-start.42
  298.8 2.6 collective-permute-done.42
  306.0 4.8 %multiply_reduce_fusion = (f32[1024]{0:T(1024)S(1)}, f32[1024]{0:T(1024)S(1)}, f32[1024]{0:T(1024)S(1)}, f32[1024]{0:T(1024)S(1)}) fusion(bf16[1024,1024]{1,0:T(8,128)(2,1)} %collective-permute-done.9, bf16[1024,1024]{1,0:T(8,128)(2,1)} %get-tuple-element.27, f32[1024,1024]{1,0:T(8,128)} %copy-done.1, f32[1024]{0:T(1024)S(1)} %add_rsqrt_fusion, ...), kind=kLoop, calls=%fused_computation.17 | loop fusion | flops 12578816 | bytes 8417280 | tf_op jit(solution)/shard_map/reduce_sum | solution.py:459
  311.3 5.3 %convert_reduce_fusion.1 = (f32[1024]{0:T(1024)S(1)}, bf16[1024,1024]{1,0:T(8,128)(2,1)}, f32[1024,1024]{1,0:T(8,128)}) fusion(f32[1024]{0:T(1024)S(1)} %get-tuple-element.188, f32[1024,1024]{1,0:T(8,128)S(1)} %copy-done.2, f32[1024]{0:T(1024)S(1)} %broadcast_multiply_fusion.8, f32[1024]{0:T(1024)S(1)} %get-tuple-element.189, ...), kind=kLoop, calls=%fused_computation.18 | loop fusion | flops 15727616 | bytes 16801792 | tf_op jit(solution)/shard_map/reduce_sum | solution.py:458
  316.6 4.5 reshape.939
  321.1 3.9 convolution_convert_fusion.5.do_ref
  324.9 26.1 %attend_back.1 = (bf16[1024,512]{1,0:T(8,128)(2,1)}, bf16[1024,512]{1,0:T(8,128)(2,1)}, bf16[1024,512]{1,0:T(8,128)(2,1)}) custom-call(bf16[1024,512]{1,0:T(8,128)(2,1)} %get-tuple-element.94.q_ref, bf16[1024,512]{1,0:T(8,128)(2,1)} %slice.172.k_ref, bf16[1024,512]{1,0:T(8,128)(2,1)} %get-tuple-element.93.v_ref, ...), custom_call_target="tpu_custom_call" | custom-call | tf_op jit(solution)/shard_map/attend_back/pallas_call | solution.py:150
  362.4 4.7 %convolution_convert_fusion.3 = bf16[1024,1024]{1,0:T(8,128)(2,1)} fusion(bf16[1024,1536]{1,0:T(8,128)(2,1)S(1)} %constant_dynamic-update-slice_fusion, bf16[1024,1536]{0,1:T(8,128)(2,1)S(1)} %bitcast.614), kind=kOutput, calls=%fused_computation.62 | convolution fusion | flops 3222274048 | bytes 8388608 | tf_op jit(solution)/shard_map/dot_general | solution.py:25
  367.1 4.1 convolution_convert_fusion
  372.5 2.6 collective-permute-start.17
  393.0 2.4 collective-permute-done.25
  396.7 3.1 collective-permute-done.31
  401.7 3.8 collective-permute-done.18
  405.8 2.5 collective-permute-start.23
  408.2 6.6 %collective-permute-done.26 = bf16[2,2,64,512]{3,2,1,0:T(8,128)(2,1)S(1)} collective-permute-done((bf16[2,2,64,512]{3,2,1,0:T(8,128)(2,1)S(1)}, bf16[2,2,64,512]{3,2,1,0:T(8,128)(2,1)S(1)}, u32[]{:S(2)}, u32[]{:S(2)}) %collective-permute-start.26) | collective-permute-done | bytes 262176 | tf_op jit(solution)/shard_map/ppermute | solution.py:330
  426.2 2.5 fusion.25
  430.7 2.4 collective-permute-done.12
  434.7 3.4 fusion.24
  449.2 3.8 collective-permute-done.15
  (356 shorter events, 124.2 us)
Async XLA Ops:
  3.1 74.6 %collective-permute-start = (bf16[256,1024]{1,0:T(8,128)(2,1)}, bf16[256,1024]{1,0:T(8,128)(2,1)}, u32[]{:S(2)}, u32[]{:S(2)}) collective-permute-start(bf16[256,1024]{1,0:T(8,128)(2,1)} %get-tuple-element.136), channel_id=1, source_target_pairs={{0,1},{1,0},{2,3},{3,2},{4,5},{5,4},{6,7},{7,6},{8,9},{9,8},{10,11... | collective-permute-start | bytes 1572872 | tf_op jit(solution)/shard_map/ppermute | solution.py:300
  3.6 73.6 %collective-permute-start.1 = (bf16[256,1024]{1,0:T(8,128)(2,1)}, bf16[256,1024]{1,0:T(8,128)(2,1)}, u32[]{:S(2)}, u32[]{:S(2)}) collective-permute-start(bf16[256,1024]{1,0:T(8,128)(2,1)} %get-tuple-element.137), channel_id=1, source_target_pairs={{0,2},{1,3},{2,0},{3,1},{4,6},{5,7},{6,4},{7,5},{8,10},{9,11},{10,... | collective-permute-start | bytes 1572872 | tf_op jit(solution)/shard_map/ppermute | solution.py:294
  7.1 70.3 %collective-permute-start.5 = (bf16[256,1024]{1,0:T(8,128)(2,1)}, bf16[256,1024]{1,0:T(8,128)(2,1)}, u32[]{:S(2)}, u32[]{:S(2)}) collective-permute-start(bf16[256,1024]{1,0:T(8,128)(2,1)} %get-tuple-element.131), channel_id=1, source_target_pairs={{0,2},{1,3},{2,0},{3,1},{4,6},{5,7},{6,4},{7,5},{8,10},{9,11},{10,... | collective-permute-start | bytes 1572872 | tf_op jit(solution)/shard_map/ppermute | solution.py:294
  7.1 71.8 %collective-permute-start.4 = (bf16[256,1024]{1,0:T(8,128)(2,1)}, bf16[256,1024]{1,0:T(8,128)(2,1)}, u32[]{:S(2)}, u32[]{:S(2)}) collective-permute-start(bf16[256,1024]{1,0:T(8,128)(2,1)} %get-tuple-element.130), channel_id=1, source_target_pairs={{0,1},{1,0},{2,3},{3,2},{4,5},{5,4},{6,7},{7,6},{8,9},{9,8},{10,11... | collective-permute-start | bytes 1572872 | tf_op jit(solution)/shard_map/ppermute | solution.py:300
  77.4 48.7 %collective-permute-start.6 = (bf16[256,1024]{1,0:T(8,128)(2,1)}, bf16[256,1024]{1,0:T(8,128)(2,1)S(1)}, u32[]{:S(2)}, u32[]{:S(2)}) collective-permute-start(bf16[256,1024]{1,0:T(8,128)(2,1)} %collective-permute-done.5), channel_id=1, source_target_pairs={{0,1},{1,0},{2,3},{3,2},{4,5},{5,4},{6,7},{7,6},{8,9},{9,8},{10,11... | collective-permute-start | bytes 1572872 | tf_op jit(solution)/shard_map/ppermute | solution.py:300
  125.1 6.5 %collective-permute-start.3 = (bf16[1024,512]{1,0:T(8,128)(2,1)}, bf16[1024,512]{1,0:T(8,128)(2,1)S(1)}, u32[]{:S(2)}, u32[]{:S(2)}) collective-permute-start(bf16[1024,512]{1,0:T(8,128)(2,1)} %get-tuple-element.25.mixed_ref), channel_id=1, source_target_pairs={{0,1},{1,0},{2,3},{3,2},{4,5},{5,4},{6,7},{7,6},{8,9},{9,8},{10,11... | collective-permute-start | bytes 3145736 | tf_op jit(solution)/shard_map/ppermute | solution.py:300
  188.9 41.8 %collective-permute-start.48 = (bf16[2,2,2,128,384]{4,3,2,0,1:T(8,128)(2,1)S(1)}, bf16[2,2,2,128,384]{4,3,2,0,1:T(8,128)(2,1)S(1)}, u32[]{:S(2)}, u32[]{:S(2)}) collective-permute-start(bf16[2,2,2,128,384]{4,3,2,0,1:T(8,128)(2,1)S(1)} %copy_bitcast_fusion.4), channel_id=1, source_target_pairs={{0,4},{4,0},{8,12},{12,8},{16,20},{20,16},{24,28},{28,24},{1,5},{5... | collective-permute-start | bytes 2359304 | tf_op jit(solution)/shard_map/ppermute | solution.py:330
  191.1 55.0 %collective-permute-start.52 = (bf16[2,2,2,128,384]{4,3,1,0,2:T(8,128)(2,1)S(1)}, bf16[2,2,2,128,384]{4,3,1,0,2:T(8,128)(2,1)S(1)}, u32[]{:S(2)}, u32[]{:S(2)}) collective-permute-start(bf16[2,2,2,128,384]{4,3,1,0,2:T(8,128)(2,1)S(1)} %copy_bitcast_fusion.3), channel_id=1, source_target_pairs={{0,2},{1,3},{2,0},{3,1},{4,6},{5,7},{6,4},{7,5},{8,10},{9,11},{10,... | collective-permute-start | bytes 2359304 | tf_op jit(solution)/shard_map/ppermute | solution.py:294
  192.7 14.9 %collective-permute-start.56 = (bf16[2,2,2,128,256]{4,3,2,1,0:T(8,128)(2,1)S(1)}, bf16[2,2,2,128,256]{4,3,2,1,0:T(8,128)(2,1)S(1)}, u32[]{:S(2)}, u32[]{:S(2)}) collective-permute-start(bf16[2,2,2,128,256]{4,3,2,1,0:T(8,128)(2,1)S(1)} %dynamic-slice_bitcast_fusion.2), channel_id=1, source_target_pairs={{0,8},{4,12},{8,0},{12,4},{16,24},{20,28},{24,16},{28,20},{1,9},{5... | collective-permute-start | bytes 1572872 | tf_op jit(solution)/shard_map/ppermute | solution.py:330
  194.4 23.0 %collective-permute-start.43 = (bf16[2,2,2,64,512]{4,3,2,1,0:T(8,128)(2,1)S(1)}, bf16[2,2,2,64,512]{4,3,2,1,0:T(8,128)(2,1)S(1)}, u32[]{:S(2)}, u32[]{:S(2)}) collective-permute-start(bf16[2,2,2,64,512]{4,3,2,1,0:T(8,128)(2,1)S(1)} %dynamic-slice_bitcast_fusion.3), channel_id=1, source_target_pairs={{0,8},{4,12},{8,0},{12,4},{16,24},{20,28},{24,16},{28,20},{1,9},{5... | collective-permute-start | bytes 1572872 | tf_op jit(solution)/shard_map/ppermute | solution.py:330
  194.9 36.1 %collective-permute-start.35 = (bf16[2,2,2,64,768]{4,3,2,0,1:T(8,128)(2,1)S(1)}, bf16[2,2,2,64,768]{4,3,2,0,1:T(8,128)(2,1)S(1)}, u32[]{:S(2)}, u32[]{:S(2)}) collective-permute-start(bf16[2,2,2,64,768]{4,3,2,0,1:T(8,128)(2,1)S(1)} %copy_bitcast_fusion.6), channel_id=1, source_target_pairs={{0,4},{4,0},{8,12},{12,8},{16,20},{20,16},{24,28},{28,24},{1,5},{5... | collective-permute-start | bytes 2359304 | tf_op jit(solution)/shard_map/ppermute | solution.py:330
  207.6 39.3 %collective-permute-start.39 = (bf16[2,2,2,64,768]{4,3,1,0,2:T(8,128)(2,1)S(1)}, bf16[2,2,2,64,768]{4,3,1,0,2:T(8,128)(2,1)S(1)}, u32[]{:S(2)}, u32[]{:S(2)}) collective-permute-start(bf16[2,2,2,64,768]{4,3,1,0,2:T(8,128)(2,1)S(1)} %copy_bitcast_fusion.5), channel_id=1, source_target_pairs={{0,2},{1,3},{2,0},{3,1},{4,6},{5,7},{6,4},{7,5},{8,10},{9,11},{10,... | collective-permute-start | bytes 2359304 | tf_op jit(solution)/shard_map/ppermute | solution.py:294
  217.3 13.3 %collective-permute-start.57 = (bf16[2,2,128,256]{3,2,1,0:T(8,128)(2,1)S(1)}, bf16[2,2,128,256]{3,2,1,0:T(8,128)(2,1)S(1)}, u32[]{:S(2)}, u32[]{:S(2)}) collective-permute-start(bf16[2,2,128,256]{3,2,1,0:T(8,128)(2,1)S(1)} %get-tuple-element.113), channel_id=1, source_target_pairs={{0,16},{4,20},{8,24},{12,28},{16,0},{20,4},{24,8},{28,12},{1,17},{... | collective-permute-start | bytes 786440 | tf_op jit(solution)/shard_map/ppermute | solution.py:330
  230.7 75.4 %collective-permute-start.9 = (bf16[1024,1024]{1,0:T(8,128)(2,1)}, bf16[1024,1024]{1,0:T(8,128)(2,1)}, u32[]{:S(2)}, u32[]{:S(2)}) collective-permute-start(bf16[1024,1024]{1,0:T(8,128)(2,1)} %get-tuple-element.27), channel_id=1, source_target_pairs={{0,1},{1,0},{2,3},{3,2},{4,5},{5,4},{6,7},{7,6},{8,9},{9,8},{10,11... | collective-permute-start | bytes 6291464 | tf_op jit(solution)/shard_map/ppermute | solution.py:300
  230.7 15.3 %collective-permute-start.44 = (bf16[2,2,64,512]{3,2,1,0:T(8,128)(2,1)S(1)}, bf16[2,2,64,512]{3,2,1,0:T(8,128)(2,1)S(1)}, u32[]{:S(2)}, u32[]{:S(2)}) collective-permute-start(bf16[2,2,64,512]{3,2,1,0:T(8,128)(2,1)S(1)} %get-tuple-element.115), channel_id=1, source_target_pairs={{0,16},{4,20},{8,24},{12,28},{16,0},{20,4},{24,8},{28,12},{1,17},{... | collective-permute-start | bytes 786440 | tf_op jit(solution)/shard_map/ppermute | solution.py:330
  231.1 34.8 %collective-permute-start.7 = (bf16[2,256,1024]{2,1,0:T(8,128)(2,1)S(1)}, bf16[2,256,1024]{2,1,0:T(8,128)(2,1)S(1)}, u32[]{:S(2)}, u32[]{:S(2)}) collective-permute-start(bf16[2,256,1024]{2,1,0:T(8,128)(2,1)S(1)} %dynamic-slice_bitcast_fusion.1), channel_id=1, source_target_pairs={{0,1},{1,0},{2,3},{3,2},{4,5},{5,4},{6,7},{7,6},{8,9},{9,8},{10,11... | collective-permute-start | bytes 3145736 | tf_op jit(solution)/shard_map/ppermute | solution.py:300
  246.0 21.3 %collective-permute-start.49 = (bf16[2,2,128,384]{3,2,1,0:T(8,128)(2,1)S(1)}, bf16[2,2,128,384]{3,2,1,0:T(8,128)(2,1)S(1)}, u32[]{:S(2)}, u32[]{:S(2)}) collective-permute-start(bf16[2,2,128,384]{3,2,1,0:T(8,128)(2,1)S(1)} %get-tuple-element.103), channel_id=1, source_target_pairs={{0,8},{4,12},{8,0},{12,4},{16,24},{20,28},{24,16},{28,20},{1,9},{5... | collective-permute-start | bytes 1179656 | tf_op jit(solution)/shard_map/ppermute | solution.py:330
  246.1 6.5 %collective-permute-start.58 = (bf16[2,128,256]{2,1,0:T(8,128)(2,1)S(1)}, bf16[2,128,256]{2,1,0:T(8,128)(2,1)S(1)}, u32[]{:S(2)}, u32[]{:S(2)}) collective-permute-start(bf16[2,128,256]{2,1,0:T(8,128)(2,1)S(1)} %get-tuple-element.151), channel_id=1, source_target_pairs={{0,4},{4,0},{8,12},{12,8},{16,20},{20,16},{24,28},{28,24},{1,5},{5... | collective-permute-start | bytes 393224 | tf_op jit(solution)/shard_map/ppermute | solution.py:330
  246.9 8.5 %collective-permute-start.45 = (bf16[2,64,512]{2,1,0:T(8,128)(2,1)S(1)}, bf16[2,64,512]{2,1,0:T(8,128)(2,1)S(1)}, u32[]{:S(2)}, u32[]{:S(2)}) collective-permute-start(bf16[2,64,512]{2,1,0:T(8,128)(2,1)S(1)} %get-tuple-element.153), channel_id=1, source_target_pairs={{0,4},{4,0},{8,12},{12,8},{16,20},{20,16},{24,28},{28,24},{1,5},{5... | collective-permute-start | bytes 393224 | tf_op jit(solution)/shard_map/ppermute | solution.py:330
  252.6 15.4 %collective-permute-start.53 = (bf16[2,2,128,384]{3,2,1,0:T(8,128)(2,1)S(1)}, bf16[2,2,128,384]{3,2,1,0:T(8,128)(2,1)S(1)}, u32[]{:S(2)}, u32[]{:S(2)}) collective-permute-start(bf16[2,2,128,384]{3,2,1,0:T(8,128)(2,1)S(1)} %get-tuple-element.105), channel_id=1, source_target_pairs={{0,4},{4,0},{8,12},{12,8},{16,20},{20,16},{24,28},{28,24},{1,5},{5... | collective-permute-start | bytes 1179656 | tf_op jit(solution)/shard_map/ppermute | solution.py:330
  264.6 14.1 %collective-permute-start.36 = (bf16[2,2,64,768]{3,2,1,0:T(8,128)(2,1)S(1)}, bf16[2,2,64,768]{3,2,1,0:T(8,128)(2,1)S(1)}, u32[]{:S(2)}, u32[]{:S(2)}) collective-permute-start(bf16[2,2,64,768]{3,2,1,0:T(8,128)(2,1)S(1)} %get-tuple-element.107), channel_id=1, source_target_pairs={{0,8},{4,12},{8,0},{12,4},{16,24},{20,28},{24,16},{28,20},{1,9},{5... | collective-permute-start | bytes 1179656 | tf_op jit(solution)/shard_map/ppermute | solution.py:330
  265.9 13.0 %collective-permute-start.40 = (bf16[2,2,64,768]{3,2,1,0:T(8,128)(2,1)S(1)}, bf16[2,2,64,768]{3,2,1,0:T(8,128)(2,1)S(1)}, u32[]{:S(2)}, u32[]{:S(2)}) collective-permute-start(bf16[2,2,64,768]{3,2,1,0:T(8,128)(2,1)S(1)} %get-tuple-element.109), channel_id=1, source_target_pairs={{0,4},{4,0},{8,12},{12,8},{16,20},{20,16},{24,28},{28,24},{1,5},{5... | collective-permute-start | bytes 1179656 | tf_op jit(solution)/shard_map/ppermute | solution.py:330
  267.4 35.1 %collective-permute-start.8 = (bf16[256,1024]{1,0:T(8,128)(2,1)S(1)}, bf16[256,1024]{1,0:T(8,128)(2,1)S(1)}, u32[]{:S(2)}, u32[]{:S(2)}) collective-permute-start(bf16[256,1024]{1,0:T(8,128)(2,1)S(1)} %slice_bitcast_fusion.2), channel_id=1, source_target_pairs={{0,2},{1,3},{2,0},{3,1},{4,6},{5,7},{6,4},{7,5},{8,10},{9,11},{10,... | collective-permute-start | bytes 1572872 | tf_op jit(solution)/shard_map/ppermute | solution.py:294
  268.0 13.8 %collective-permute-start.50 = (bf16[2,128,384]{2,1,0:T(8,128)(2,1)S(1)}, bf16[2,128,384]{2,1,0:T(8,128)(2,1)S(1)}, u32[]{:S(2)}, u32[]{:S(2)}) collective-permute-start(bf16[2,128,384]{2,1,0:T(8,128)(2,1)S(1)} %get-tuple-element.141), channel_id=1, source_target_pairs={{0,16},{4,20},{8,24},{12,28},{16,0},{20,4},{24,8},{28,12},{1,17},{... | collective-permute-start | bytes 589832 | tf_op jit(solution)/shard_map/ppermute | solution.py:330
  278.8 7.2 %collective-permute-start.54 = (bf16[2,128,384]{2,1,0:T(8,128)(2,1)S(1)}, bf16[2,128,384]{2,1,0:T(8,128)(2,1)S(1)}, u32[]{:S(2)}, u32[]{:S(2)}) collective-permute-start(bf16[2,128,384]{2,1,0:T(8,128)(2,1)S(1)} %get-tuple-element.143), channel_id=1, source_target_pairs={{0,8},{4,12},{8,0},{12,4},{16,24},{20,28},{24,16},{28,20},{1,9},{5... | collective-permute-start | bytes 589832 | tf_op jit(solution)/shard_map/ppermute | solution.py:330
  278.9 12.0 %collective-permute-start.37 = (bf16[2,64,768]{2,1,0:T(8,128)(2,1)S(1)}, bf16[2,64,768]{2,1,0:T(8,128)(2,1)S(1)}, u32[]{:S(2)}, u32[]{:S(2)}) collective-permute-start(bf16[2,64,768]{2,1,0:T(8,128)(2,1)S(1)} %get-tuple-element.145), channel_id=1, source_target_pairs={{0,16},{4,20},{8,24},{12,28},{16,0},{20,4},{24,8},{28,12},{1,17},{... | collective-permute-start | bytes 589832 | tf_op jit(solution)/shard_map/ppermute | solution.py:330
  281.8 9.2 %collective-permute-start.41 = (bf16[2,64,768]{2,1,0:T(8,128)(2,1)S(1)}, bf16[2,64,768]{2,1,0:T(8,128)(2,1)S(1)}, u32[]{:S(2)}, u32[]{:S(2)}) collective-permute-start(bf16[2,64,768]{2,1,0:T(8,128)(2,1)S(1)} %get-tuple-element.147), channel_id=1, source_target_pairs={{0,8},{4,12},{8,0},{12,4},{16,24},{20,28},{24,16},{28,20},{1,9},{5... | collective-permute-start | bytes 589832 | tf_op jit(solution)/shard_map/ppermute | solution.py:330
  285.9 15.6 %collective-permute-start.51 = (bf16[128,384]{1,0:T(8,128)(2,1)S(1)}, bf16[128,384]{1,0:T(8,128)(2,1)S(1)}, u32[]{:S(2)}, u32[]{:S(2)}) collective-permute-start(bf16[128,384]{1,0:T(8,128)(2,1)S(1)} %fusion.94), channel_id=1, source_target_pairs={{0,2},{1,3},{2,0},{3,1},{4,6},{5,7},{6,4},{7,5},{8,10},{9,11},{10,... | collective-permute-start | bytes 294920 | tf_op jit(solution)/shard_map/ppermute | solution.py:294
  290.9 10.7 %collective-permute-start.55 = (bf16[128,384]{1,0:T(8,128)(2,1)S(1)}, bf16[128,384]{1,0:T(8,128)(2,1)S(1)}, u32[]{:S(2)}, u32[]{:S(2)}) collective-permute-start(bf16[128,384]{1,0:T(8,128)(2,1)S(1)} %fusion.96), channel_id=1, source_target_pairs={{0,16},{4,20},{8,24},{12,28},{16,0},{20,4},{24,8},{28,12},{1,17},{... | collective-permute-start | bytes 294920 | tf_op jit(solution)/shard_map/ppermute | solution.py:330
  295.8 5.5 %collective-permute-start.42 = (bf16[64,768]{1,0:T(8,128)(2,1)S(1)}, bf16[64,768]{1,0:T(8,128)(2,1)S(1)}, u32[]{:S(2)}, u32[]{:S(2)}) collective-permute-start(bf16[64,768]{1,0:T(8,128)(2,1)S(1)} %fusion.92), channel_id=1, source_target_pairs={{0,16},{4,20},{8,24},{12,28},{16,0},{20,4},{24,8},{28,12},{1,17},{... | collective-permute-start | bytes 294920 | tf_op jit(solution)/shard_map/ppermute | solution.py:330
  358.2 24.4 %collective-permute-start.30 = (bf16[2,2,2,64,512]{4,3,2,1,0:T(8,128)(2,1)}, bf16[2,2,2,64,512]{4,3,2,1,0:T(8,128)(2,1)}, u32[]{:S(2)}, u32[]{:S(2)}) collective-permute-start(bf16[2,2,2,64,512]{4,3,2,1,0:T(8,128)(2,1)} %dynamic-slice_bitcast_fusion.4), channel_id=1, source_target_pairs={{0,8},{4,12},{8,0},{12,4},{16,24},{20,28},{24,16},{28,20},{1,9},{5... | collective-permute-start | bytes 1572872 | tf_op jit(solution)/shard_map/ppermute | solution.py:330
  372.5 15.2 %collective-permute-start.17 = (bf16[2,2,2,64,512]{4,3,2,0,1:T(8,128)(2,1)}, bf16[2,2,2,64,512]{4,3,2,0,1:T(8,128)(2,1)}, u32[]{:S(2)}, u32[]{:S(2)}) collective-permute-start(bf16[2,2,2,64,512]{4,3,2,0,1:T(8,128)(2,1)} %copy_bitcast_fusion.8), channel_id=1, source_target_pairs={{0,4},{4,0},{8,12},{12,8},{16,20},{20,16},{24,28},{28,24},{1,5},{5... | collective-permute-start | bytes 1572872 | tf_op jit(solution)/shard_map/ppermute | solution.py:330
  375.9 14.2 %collective-permute-start.21 = (bf16[2,2,2,64,512]{4,3,1,0,2:T(8,128)(2,1)}, bf16[2,2,2,64,512]{4,3,1,0,2:T(8,128)(2,1)}, u32[]{:S(2)}, u32[]{:S(2)}) collective-permute-start(bf16[2,2,2,64,512]{4,3,1,0,2:T(8,128)(2,1)} %copy_bitcast_fusion.7), channel_id=1, source_target_pairs={{0,2},{1,3},{2,0},{3,1},{4,6},{5,7},{6,4},{7,5},{8,10},{9,11},{10,... | collective-permute-start | bytes 1572872 | tf_op jit(solution)/shard_map/ppermute | solution.py:294
  376.7 18.7 %collective-permute-start.25 = (bf16[2,2,2,64,512]{4,3,2,1,0:T(8,128)(2,1)}, bf16[2,2,2,64,512]{4,3,2,1,0:T(8,128)(2,1)}, u32[]{:S(2)}, u32[]{:S(2)}) collective-permute-start(bf16[2,2,2,64,512]{4,3,2,1,0:T(8,128)(2,1)} %dynamic-slice_bitcast_fusion.5), channel_id=1, source_target_pairs={{0,8},{4,12},{8,0},{12,4},{16,24},{20,28},{24,16},{28,20},{1,9},{5... | collective-permute-start | bytes 1572872 | tf_op jit(solution)/shard_map/ppermute | solution.py:330
  381.3 44.9 %collective-permute-start.10 = (bf16[2,256,1024]{2,1,0:T(8,128)(2,1)}, bf16[2,256,1024]{2,1,0:T(8,128)(2,1)}, u32[]{:S(2)}, u32[]{:S(2)}) collective-permute-start(bf16[2,256,1024]{2,1,0:T(8,128)(2,1)} %dynamic-slice_bitcast_fusion), channel_id=1, source_target_pairs={{0,1},{1,0},{2,3},{3,2},{4,5},{5,4},{6,7},{7,6},{8,9},{9,8},{10,11... | collective-permute-start | bytes 3145736 | tf_op jit(solution)/shard_map/ppermute | solution.py:300
  384.0 15.8 %collective-permute-start.31 = (bf16[2,2,64,512]{3,2,1,0:T(8,128)(2,1)S(1)}, bf16[2,2,64,512]{3,2,1,0:T(8,128)(2,1)S(1)}, u32[]{:S(2)}, u32[]{:S(2)}) collective-permute-start(bf16[2,2,64,512]{3,2,1,0:T(8,128)(2,1)S(1)} %get-tuple-element.117), channel_id=1, source_target_pairs={{0,16},{4,20},{8,24},{12,28},{16,0},{20,4},{24,8},{28,12},{1,17},{... | collective-permute-start | bytes 786440 | tf_op jit(solution)/shard_map/ppermute | solution.py:330
  389.0 16.6 %collective-permute-start.18 = (bf16[2,2,64,512]{3,2,1,0:T(8,128)(2,1)S(1)}, bf16[2,2,64,512]{3,2,1,0:T(8,128)(2,1)S(1)}, u32[]{:S(2)}, u32[]{:S(2)}) collective-permute-start(bf16[2,2,64,512]{3,2,1,0:T(8,128)(2,1)S(1)} %get-tuple-element.119), channel_id=1, source_target_pairs={{0,8},{4,12},{8,0},{12,4},{16,24},{20,28},{24,16},{28,20},{1,9},{5... | collective-permute-start | bytes 786440 | tf_op jit(solution)/shard_map/ppermute | solution.py:330
  391.2 14.4 %collective-permute-start.22 = (bf16[2,2,64,512]{3,2,1,0:T(8,128)(2,1)S(1)}, bf16[2,2,64,512]{3,2,1,0:T(8,128)(2,1)S(1)}, u32[]{:S(2)}, u32[]{:S(2)}) collective-permute-start(bf16[2,2,64,512]{3,2,1,0:T(8,128)(2,1)S(1)} %get-tuple-element.121), channel_id=1, source_target_pairs={{0,4},{4,0},{8,12},{12,8},{16,20},{20,16},{24,28},{28,24},{1,5},{5... | collective-permute-start | bytes 786440 | tf_op jit(solution)/shard_map/ppermute | solution.py:330
  396.6 18.2 %collective-permute-start.26 = (bf16[2,2,64,512]{3,2,1,0:T(8,128)(2,1)S(1)}, bf16[2,2,64,512]{3,2,1,0:T(8,128)(2,1)S(1)}, u32[]{:S(2)}, u32[]{:S(2)}) collective-permute-start(bf16[2,2,64,512]{3,2,1,0:T(8,128)(2,1)S(1)} %get-tuple-element.123), channel_id=1, source_target_pairs={{0,16},{4,20},{8,24},{12,28},{16,0},{20,4},{24,8},{28,12},{1,17},{... | collective-permute-start | bytes 786440 | tf_op jit(solution)/shard_map/ppermute | solution.py:330
  399.9 16.5 %collective-permute-start.32 = (bf16[2,64,512]{2,1,0:T(8,128)(2,1)S(1)}, bf16[2,64,512]{2,1,0:T(8,128)(2,1)S(1)}, u32[]{:S(2)}, u32[]{:S(2)}) collective-permute-start(bf16[2,64,512]{2,1,0:T(8,128)(2,1)S(1)} %get-tuple-element.155), channel_id=1, source_target_pairs={{0,4},{4,0},{8,12},{12,8},{16,20},{20,16},{24,28},{28,24},{1,5},{5... | collective-permute-start | bytes 393224 | tf_op jit(solution)/shard_map/ppermute | solution.py:330
  405.6 11.7 %collective-permute-start.19 = (bf16[2,64,512]{2,1,0:T(8,128)(2,1)S(1)}, bf16[2,64,512]{2,1,0:T(8,128)(2,1)S(1)}, u32[]{:S(2)}, u32[]{:S(2)}) collective-permute-start(bf16[2,64,512]{2,1,0:T(8,128)(2,1)S(1)} %get-tuple-element.157), channel_id=1, source_target_pairs={{0,16},{4,20},{8,24},{12,28},{16,0},{20,4},{24,8},{28,12},{1,17},{... | collective-permute-start | bytes 393224 | tf_op jit(solution)/shard_map/ppermute | solution.py:330
  405.8 12.9 %collective-permute-start.23 = (bf16[2,64,512]{2,1,0:T(8,128)(2,1)S(1)}, bf16[2,64,512]{2,1,0:T(8,128)(2,1)S(1)}, u32[]{:S(2)}, u32[]{:S(2)}) collective-permute-start(bf16[2,64,512]{2,1,0:T(8,128)(2,1)S(1)} %get-tuple-element.159), channel_id=1, source_target_pairs={{0,8},{4,12},{8,0},{12,4},{16,24},{20,28},{24,16},{28,20},{1,9},{5... | collective-permute-start | bytes 393224 | tf_op jit(solution)/shard_map/ppermute | solution.py:330
  414.9 5.0 %collective-permute-start.27 = (bf16[2,64,512]{2,1,0:T(8,128)(2,1)S(1)}, bf16[2,64,512]{2,1,0:T(8,128)(2,1)S(1)}, u32[]{:S(2)}, u32[]{:S(2)}) collective-permute-start(bf16[2,64,512]{2,1,0:T(8,128)(2,1)S(1)} %get-tuple-element.161), channel_id=1, source_target_pairs={{0,4},{4,0},{8,12},{12,8},{16,20},{20,16},{24,28},{28,24},{1,5},{5... | collective-permute-start | bytes 393224 | tf_op jit(solution)/shard_map/ppermute | solution.py:330
  416.4 5.4 %collective-permute-start.33 = (bf16[64,512]{1,0:T(8,128)(2,1)S(1)}, bf16[64,512]{1,0:T(8,128)(2,1)S(1)}, u32[]{:S(2)}, u32[]{:S(2)}) collective-permute-start(bf16[64,512]{1,0:T(8,128)(2,1)S(1)} %fusion.105), channel_id=1, source_target_pairs={{0,2},{1,3},{2,0},{3,1},{4,6},{5,7},{6,4},{7,5},{8,10},{9,11},{10,... | collective-permute-start | bytes 196616 | tf_op jit(solution)/shard_map/ppermute | solution.py:294
  418.6 5.2 %collective-permute-start.24 = (bf16[64,512]{1,0:T(8,128)(2,1)S(1)}, bf16[64,512]{1,0:T(8,128)(2,1)S(1)}, u32[]{:S(2)}, u32[]{:S(2)}) collective-permute-start(bf16[64,512]{1,0:T(8,128)(2,1)S(1)} %fusion.101), channel_id=1, source_target_pairs={{0,16},{4,20},{8,24},{12,28},{16,0},{20,4},{24,8},{28,12},{1,17},{... | collective-permute-start | bytes 196616 | tf_op jit(solution)/shard_map/ppermute | solution.py:330
  425.1 18.8 %collective-permute-start.29 = (bf16[32,1536]{1,0:T(8,128)(2,1)}, bf16[32,1536]{1,0:T(8,128)(2,1)}, u32[]{:S(2)}, u32[]{:S(2)}) collective-permute-start(bf16[32,1536]{1,0:T(8,128)(2,1)} %fusion.88), channel_id=1, source_target_pairs={{0,1},{1,0},{2,3},{3,2},{4,5},{5,4},{6,7},{7,6},{8,9},{9,8},{10,11... | collective-permute-start | bytes 294920 | tf_op jit(solution)/shard_map/ppermute | solution.py:300
  440.1 18.1 %collective-permute-start.11 = (bf16[256,1024]{1,0:T(8,128)(2,1)}, bf16[256,1024]{1,0:T(8,128)(2,1)}, u32[]{:S(2)}, u32[]{:S(2)}) collective-permute-start(bf16[256,1024]{1,0:T(8,128)(2,1)} %slice_bitcast_fusion), channel_id=1, source_target_pairs={{0,2},{1,3},{2,0},{3,1},{4,6},{5,7},{6,4},{7,5},{8,10},{9,11},{10,... | collective-permute-start | bytes 1572872 | tf_op jit(solution)/shard_map/ppermute | solution.py:294
  443.3 9.8 %collective-permute-start.15 = (f32[2,384]{1,0:T(2,128)}, f32[2,384]{1,0:T(2,128)}, u32[]{:S(2)}, u32[]{:S(2)}) collective-permute-start(f32[2,384]{1,0:T(2,128)} %fusion.130), channel_id=1, source_target_pairs={{0,2},{1,3},{2,0},{3,1},{4,6},{5,7},{6,4},{7,5},{8,10},{9,11},{10,... | collective-permute-start | bytes 9224 | tf_op jit(solution)/shard_map/ppermute | solution.py:294
  (57 other events, 650.8 us)
